TPU v7x, 32 devices: a whole 2x2x4 slice. The times are simulated.
32 devices in a mesh: dp: 4 (over z), expert: 8 (over y, x, core).
Axes of the slice: x: 2, y: 2, z: 4, core: 2. Of those that a mesh axis runs over, the one named last changes fastest.
Arguments:
- tokens: bfloat16 [128, 197, 768], P(('dp', 'expert')), may hold values from -6 to 6
- routes: int32 [128, 197, 2], P(('dp', 'expert')), may hold values from 0 to 7, all different within a row; in each aligned block of 788 rows (0 to 787, 788 to 1575, ..., all dimensions but the last counted through in order) at most 248 rows name the same one
- gain_one: bfloat16 [768], P(('dp', 'expert')), may hold values from 0.5 to 1.5
- shift_one: bfloat16 [768], P(('dp', 'expert')), may hold values from -1.796875 to 1.796875
- w_query: bfloat16 [768, 768], P(('dp', 'expert')), may hold values from -0.21875 to 0.21875
- b_query: bfloat16 [768], P(('dp', 'expert')), may hold values from -1.796875 to 1.796875
- w_key: bfloat16 [768, 768], P(('dp', 'expert')), may hold values from -0.21875 to 0.21875
- w_value: bfloat16 [768, 768], P(('dp', 'expert')), may hold values from -0.21875 to 0.21875
- b_value: bfloat16 [768], P(('dp', 'expert')), may hold values from -1.796875 to 1.796875
- w_out: bfloat16 [768, 768], P(('dp', 'expert')), may hold values from -1.75 to 1.75
- b_out: bfloat16 [768], P(('dp', 'expert')), may hold values from -1.796875 to 1.796875
- gain_two: bfloat16 [768], P(('dp', 'expert')), may hold values from 0.5 to 1.5
- shift_two: bfloat16 [768], P(('dp', 'expert')), may hold values from -1.796875 to 1.796875
- w_router: bfloat16 [768, 8], P(('dp', 'expert')), may hold values from -0.15625 to 0.15625
- w_up: bfloat16 [8, 768, 3072], P('expert'), may hold values from -0.21875 to 0.21875
- b_up: bfloat16 [8, 3072], P('expert'), may hold values from -0.59765625 to 0.59765625
- w_down: bfloat16 [8, 3072, 768], P('expert'), may hold values from -2.390625 to 2.390625
- b_down: bfloat16 [8, 768], P('expert'), may hold values from -9 to 9
- cotangent: bfloat16 [128, 197, 768], P(('dp', 'expert')), may hold values from -6 to 6
Outputs:
- mixed: bfloat16 [128, 197, 768], P(('dp', 'expert'))
- grad_tokens: float32 [128, 197, 768], P(('dp', 'expert'))
- grad_gain_one: float32 [768], P(('dp', 'expert'))
- grad_shift_one: float32 [768], P(('dp', 'expert'))
- grad_w_query: float32 [768, 768], P(('dp', 'expert'))
- grad_b_query: float32 [768], P(('dp', 'expert'))
- grad_w_key: float32 [768, 768], P(('dp', 'expert'))
- grad_w_value: float32 [768, 768], P(('dp', 'expert'))
- grad_b_value: float32 [768], P(('dp', 'expert'))
- grad_w_out: float32 [768, 768], P(('dp', 'expert'))
- grad_b_out: float32 [768], P(('dp', 'expert'))
- grad_gain_two: float32 [768], P(('dp', 'expert'))
- grad_shift_two: float32 [768], P(('dp', 'expert'))
- grad_w_router: float32 [768, 8], P(('dp', 'expert'))
- grad_w_up: float32 [8, 768, 3072], P('expert', 'dp')
- grad_b_up: float32 [8, 3072], P('expert', 'dp')
- grad_w_down: float32 [8, 3072, 768], P('expert', 'dp')
- grad_b_down: float32 [8, 768], P('expert', 'dp')
Inputs may be any that keep to these rules, and one draw needn't show every extreme that they name: `routes`: the two experts of a token differ. Among the rows of one device no expert is named more than 248 times, and in every draw some expert is named exactly 248 times by the rows of some device.
All inputs are finite; a program needn't handle non-finite values.
Results may differ from a plain program's by a relative error of at most 0.015.
Values may be sent and summed in bfloat16 or wider, within the bound.
No kernel may reach another device: no remote copies, remote signals or barrier semaphores. Data moves between devices by JAX's collectives and lax.ppermute only.
A program may use at most 256 MiB of HBM per device.

v0:
```python
import jax
import jax.numpy as jnp
from jax import lax
from jax.sharding import PartitionSpec as P

HEADS = 12
HEAD_DIM = 64


highest = lax.Precision.HIGHEST
epsilon = 1e-06


def layer_norm(values, gain, shift):
    center = values - jnp.mean(values, axis=-1, keepdims=True)
    spread = jnp.mean(center * center, axis=-1, keepdims=True)
    return center * lax.rsqrt(spread + epsilon) * gain + shift


def gelu_exact(values):
    return jax.nn.gelu(values, approximate=False)


def matmul(left, right):
    return jnp.dot(left, right, preferred_element_type=jnp.float32)


def merge_lead(values):
    return values.reshape(-1, values.shape[2], values.shape[3])


def per_device(
    tokens,
    routes,
    gain_one,
    shift_one,
    w_query,
    b_query,
    w_key,
    w_value,
    b_value,
    w_out,
    b_out,
    gain_two,
    shift_two,
    w_router,
    w_up,
    b_up,
    w_down,
    b_down,
    cotangent,
):
    dense = (
        lax.all_gather(gain_one, ("dp", "expert"), axis=0, tiled=True),
        lax.all_gather(shift_one, ("dp", "expert"), axis=0, tiled=True),
        lax.all_gather(w_query, ("dp", "expert"), axis=0, tiled=True),
        lax.all_gather(b_query, ("dp", "expert"), axis=0, tiled=True),
        lax.all_gather(w_key, ("dp", "expert"), axis=0, tiled=True),
        lax.all_gather(w_value, ("dp", "expert"), axis=0, tiled=True),
        lax.all_gather(b_value, ("dp", "expert"), axis=0, tiled=True),
        lax.all_gather(w_out, ("dp", "expert"), axis=0, tiled=True),
        lax.all_gather(b_out, ("dp", "expert"), axis=0, tiled=True),
        lax.all_gather(gain_two, ("dp", "expert"), axis=0, tiled=True),
        lax.all_gather(shift_two, ("dp", "expert"), axis=0, tiled=True),
        lax.all_gather(w_router, ("dp", "expert"), axis=0, tiled=True),
    )
    (
        full_gain_one,
        full_shift_one,
        full_query,
        full_bias_query,
        full_key,
        full_value,
        full_bias_value,
        full_out,
        full_bias_out,
        full_gain_two,
        full_shift_two,
        full_router,
    ) = dense
    images, seq_len, width = tokens.shape
    rows = images * seq_len
    local_experts = w_up.shape[0]
    hidden_units = w_up.shape[2]
    experts = local_experts * lax.axis_size("expert")
    capacity = max((rows * 10 // (4 * experts) + 7) // 8 * 8, 8)
    scale = HEAD_DIM ** (-0.5)
    heads_shape = (images, seq_len, HEADS, HEAD_DIM)
    inputs = tokens.astype(jnp.float32).reshape(rows, width)
    normed = layer_norm(
        inputs, full_gain_one.astype(jnp.float32), full_shift_one.astype(jnp.float32)
    )
    normed_low = normed.astype(jnp.bfloat16)
    query = (
        (matmul(normed_low, full_query) + full_bias_query.astype(jnp.float32))
        .astype(jnp.bfloat16)
        .reshape(heads_shape)
    )
    key = matmul(normed_low, full_key).astype(jnp.bfloat16).reshape(heads_shape)
    value = (
        (matmul(normed_low, full_value) + full_bias_value.astype(jnp.float32))
        .astype(jnp.bfloat16)
        .reshape(heads_shape)
    )
    scores = jnp.einsum("bqhd,bkhd->bhqk", query, key, preferred_element_type=jnp.float32) * scale
    log_total = jax.nn.logsumexp(scores, axis=-1, keepdims=True)
    probs = jnp.exp(scores - log_total)
    attended = jnp.einsum(
        "bhqk,bkhd->bqhd", probs.astype(jnp.bfloat16), value, preferred_element_type=jnp.float32
    )
    attended = attended.reshape(rows, width).astype(jnp.bfloat16)
    resid = inputs + matmul(attended, full_out) + full_bias_out.astype(jnp.float32)
    normed_two = layer_norm(
        resid, full_gain_two.astype(jnp.float32), full_shift_two.astype(jnp.float32)
    )
    normed_two_low = normed_two.astype(jnp.bfloat16)
    logits = matmul(normed_two_low, full_router)
    gates = jax.nn.softmax(logits, axis=-1)
    flat_routes = routes.reshape(-1)
    table = (flat_routes[:, None] == jnp.arange(experts, dtype=jnp.int32)[None, :]).astype(
        jnp.int32
    )
    before = jnp.cumsum(table, axis=0) - table
    position = flat_routes * capacity + jnp.sum(before * table, axis=1)
    table_float = table.astype(jnp.float32).reshape(rows, 2, experts)
    picks = jnp.sum(gates[:, None, :] * table_float, axis=2)
    send = (
        jnp.zeros((experts * capacity, width), jnp.bfloat16)
        .at[position]
        .set(jnp.repeat(normed_two_low, 2, axis=0))
    )
    send = send.reshape(experts, capacity, width)
    arrived = lax.all_to_all(send, "expert", split_axis=0, concat_axis=0, tiled=True)
    grouped = arrived.reshape(-1, local_experts, arrived.shape[1], width)
    hidden_part = (
        jnp.einsum("secd,edf->secf", grouped, w_up, preferred_element_type=jnp.float32)
        + b_up.astype(jnp.float32)[None, :, None, :]
    )
    active_part = gelu_exact(hidden_part).astype(jnp.bfloat16)
    result_part = (
        jnp.einsum("secf,efd->secd", active_part, w_down, preferred_element_type=jnp.float32)
        + b_down.astype(jnp.float32)[None, :, None, :]
    )
    arrived, hidden, active, returned = (
        arrived,
        merge_lead(hidden_part),
        merge_lead(active_part),
        merge_lead(result_part.astype(jnp.bfloat16)),
    )
    came_back = lax.all_to_all(returned, "expert", split_axis=0, concat_axis=0, tiled=True).reshape(
        experts * capacity, width
    )
    picked = came_back[position].astype(jnp.float32).reshape(rows, 2, width)
    output = resid + jnp.sum(picks[:, :, None] * picked, axis=1)
    mixed = output.astype(jnp.bfloat16).reshape(images, seq_len, width)
    upstream = cotangent.astype(jnp.float32).reshape(rows, width)
    slot_grad = (
        (picks[:, :, None] * upstream[:, None, :]).astype(jnp.bfloat16).reshape(rows * 2, width)
    )
    pick_grad = jnp.sum(picked * upstream[:, None, :], axis=2)
    gate_grad = jnp.sum(pick_grad[:, :, None] * table_float, axis=1)
    logit_grad = gates * (gate_grad - jnp.sum(gates * gate_grad, axis=1, keepdims=True))
    grad_send = jnp.zeros((experts * capacity, width), jnp.bfloat16).at[position].set(slot_grad)
    grad_send = grad_send.reshape(experts, capacity, width)
    arrived_grad = lax.all_to_all(grad_send, "expert", split_axis=0, concat_axis=0, tiled=True)
    result_grad = arrived_grad.reshape(-1, local_experts, capacity, width)
    active_four = active.reshape(-1, local_experts, capacity, hidden_units)
    grad_w_down = jnp.einsum(
        "secf,secd->efd", active_four, result_grad, preferred_element_type=jnp.float32
    )
    grad_b_down = jnp.sum(result_grad, axis=(0, 2), dtype=jnp.float32)
    active_grad = jnp.einsum(
        "secd,efd->secf", result_grad, w_down, preferred_element_type=jnp.float32
    )
    unused, gelu_pull = jax.vjp(
        gelu_exact, hidden.reshape(-1, local_experts, capacity, hidden_units)
    )
    hidden_grad = gelu_pull(active_grad)[0].astype(jnp.bfloat16)
    arrived_four = arrived.reshape(-1, local_experts, capacity, width)
    grad_w_up = jnp.einsum(
        "secd,secf->edf", arrived_four, hidden_grad, preferred_element_type=jnp.float32
    )
    grad_b_up = jnp.sum(hidden_grad, axis=(0, 2), dtype=jnp.float32)
    entry_grad = jnp.einsum("secf,edf->secd", hidden_grad, w_up, preferred_element_type=jnp.float32)
    entry_grad = entry_grad.astype(jnp.bfloat16).reshape(-1, capacity, width)
    sent_grad = lax.all_to_all(
        entry_grad, "expert", split_axis=0, concat_axis=0, tiled=True
    ).reshape(experts * capacity, width)
    expert_sums = (
        lax.psum_scatter(
            grad_w_up.astype(jnp.bfloat16), "dp", scatter_dimension=1, tiled=True
        ).astype(jnp.float32),
        lax.psum_scatter(
            grad_b_up.astype(jnp.bfloat16), "dp", scatter_dimension=1, tiled=True
        ).astype(jnp.float32),
        lax.psum_scatter(
            grad_w_down.astype(jnp.bfloat16), "dp", scatter_dimension=1, tiled=True
        ).astype(jnp.float32),
        lax.psum_scatter(
            grad_b_down.astype(jnp.bfloat16), "dp", scatter_dimension=1, tiled=True
        ).astype(jnp.float32),
    )
    dense_back = (
        lax.all_gather(gain_one, ("dp", "expert"), axis=0, tiled=True),
        lax.all_gather(shift_one, ("dp", "expert"), axis=0, tiled=True),
        lax.all_gather(w_query, ("dp", "expert"), axis=0, tiled=True),
        lax.all_gather(b_query, ("dp", "expert"), axis=0, tiled=True),
        lax.all_gather(w_key, ("dp", "expert"), axis=0, tiled=True),
        lax.all_gather(w_value, ("dp", "expert"), axis=0, tiled=True),
        lax.all_gather(b_value, ("dp", "expert"), axis=0, tiled=True),
        lax.all_gather(w_out, ("dp", "expert"), axis=0, tiled=True),
        lax.all_gather(b_out, ("dp", "expert"), axis=0, tiled=True),
        lax.all_gather(gain_two, ("dp", "expert"), axis=0, tiled=True),
        lax.all_gather(shift_two, ("dp", "expert"), axis=0, tiled=True),
        lax.all_gather(w_router, ("dp", "expert"), axis=0, tiled=True),
    )
    (
        back_gain_one,
        back_shift_one,
        back_query,
        back_bias_query,
        back_key,
        back_value,
        back_bias_value,
        back_out,
        back_bias_out,
        back_gain_two,
        back_shift_two,
        back_router,
    ) = dense_back
    entry_sum = jnp.sum(sent_grad[position].astype(jnp.float32).reshape(rows, 2, width), axis=1)
    normed_two_grad = (
        jnp.dot(logit_grad, back_router.astype(jnp.float32).T, precision=highest) + entry_sum
    )
    grad_router = jnp.dot(normed_two_low.astype(jnp.float32).T, logit_grad, precision=highest)
    unused, norm_two_pull = jax.vjp(
        layer_norm, resid, back_gain_two.astype(jnp.float32), back_shift_two.astype(jnp.float32)
    )
    resid_from_norm, grad_gain_two, grad_shift_two = norm_two_pull(normed_two_grad)
    resid_grad = upstream + resid_from_norm
    branch_grad = resid_grad.astype(jnp.bfloat16)
    grad_b_out = jnp.sum(branch_grad, axis=0, dtype=jnp.float32)
    grad_w_out = jnp.einsum("rd,re->de", attended, branch_grad, preferred_element_type=jnp.float32)
    attended_grad = jnp.einsum(
        "re,de->rd", branch_grad, back_out, preferred_element_type=jnp.float32
    )
    attended_grad = attended_grad.astype(jnp.bfloat16).reshape(heads_shape)
    scores_again = (
        jnp.einsum("bqhd,bkhd->bhqk", query, key, preferred_element_type=jnp.float32) * scale
    )
    probs_again = jnp.exp(scores_again - log_total)
    value_grad = jnp.einsum(
        "bhqk,bqhd->bkhd",
        probs_again.astype(jnp.bfloat16),
        attended_grad,
        preferred_element_type=jnp.float32,
    )
    value_grad = value_grad.astype(jnp.bfloat16).reshape(rows, width)
    probs_grad = jnp.einsum(
        "bqhd,bkhd->bhqk", attended_grad, value, preferred_element_type=jnp.float32
    )
    score_grad = probs_again * (
        probs_grad - jnp.sum(probs_again * probs_grad, axis=-1, keepdims=True)
    )
    score_grad = score_grad.astype(jnp.bfloat16)
    query_grad = (
        (jnp.einsum("bhqk,bkhd->bqhd", score_grad, key, preferred_element_type=jnp.float32) * scale)
        .astype(jnp.bfloat16)
        .reshape(rows, width)
    )
    key_grad = (
        (
            jnp.einsum("bhqk,bqhd->bkhd", score_grad, query, preferred_element_type=jnp.float32)
            * scale
        )
        .astype(jnp.bfloat16)
        .reshape(rows, width)
    )
    grad_b_query = jnp.sum(query_grad, axis=0, dtype=jnp.float32)
    grad_b_value = jnp.sum(value_grad, axis=0, dtype=jnp.float32)
    grad_w_query = jnp.einsum(
        "rd,re->de", normed_low, query_grad, preferred_element_type=jnp.float32
    )
    grad_w_key = jnp.einsum("rd,re->de", normed_low, key_grad, preferred_element_type=jnp.float32)
    grad_w_value = jnp.einsum(
        "rd,re->de", normed_low, value_grad, preferred_element_type=jnp.float32
    )
    normed_grad = jnp.einsum(
        "re,de->rd", query_grad, back_query, preferred_element_type=jnp.float32
    )
    normed_grad = normed_grad + jnp.einsum(
        "re,de->rd", key_grad, back_key, preferred_element_type=jnp.float32
    )
    normed_grad = normed_grad + jnp.einsum(
        "re,de->rd", value_grad, back_value, preferred_element_type=jnp.float32
    )
    unused, norm_one_pull = jax.vjp(
        layer_norm, inputs, back_gain_one.astype(jnp.float32), back_shift_one.astype(jnp.float32)
    )
    input_grad, grad_gain_one, grad_shift_one = norm_one_pull(normed_grad)
    grad_tokens = (resid_grad + input_grad).reshape(images, seq_len, width)
    dense_sums = (
        lax.psum_scatter(grad_gain_one, ("dp", "expert"), scatter_dimension=0, tiled=True),
        lax.psum_scatter(grad_shift_one, ("dp", "expert"), scatter_dimension=0, tiled=True),
        lax.psum_scatter(grad_w_query, ("dp", "expert"), scatter_dimension=0, tiled=True),
        lax.psum_scatter(grad_b_query, ("dp", "expert"), scatter_dimension=0, tiled=True),
        lax.psum_scatter(grad_w_key, ("dp", "expert"), scatter_dimension=0, tiled=True),
        lax.psum_scatter(grad_w_value, ("dp", "expert"), scatter_dimension=0, tiled=True),
        lax.psum_scatter(grad_b_value, ("dp", "expert"), scatter_dimension=0, tiled=True),
        lax.psum_scatter(grad_w_out, ("dp", "expert"), scatter_dimension=0, tiled=True),
        lax.psum_scatter(grad_b_out, ("dp", "expert"), scatter_dimension=0, tiled=True),
        lax.psum_scatter(grad_gain_two, ("dp", "expert"), scatter_dimension=0, tiled=True),
        lax.psum_scatter(grad_shift_two, ("dp", "expert"), scatter_dimension=0, tiled=True),
        lax.psum_scatter(grad_router, ("dp", "expert"), scatter_dimension=0, tiled=True),
    )
    return (
        mixed,
        grad_tokens,
        dense_sums[0],
        dense_sums[1],
        dense_sums[2],
        dense_sums[3],
        dense_sums[4],
        dense_sums[5],
        dense_sums[6],
        dense_sums[7],
        dense_sums[8],
        dense_sums[9],
        dense_sums[10],
        dense_sums[11],
        expert_sums[0],
        expert_sums[1],
        expert_sums[2],
        expert_sums[3],
    )


def solution(mesh):
    return jax.shard_map(
        per_device,
        mesh=mesh,
        in_specs=(
            P(("dp", "expert"), None, None),
            P(("dp", "expert"), None, None),
            P(("dp", "expert")),
            P(("dp", "expert")),
            P(("dp", "expert"), None),
            P(("dp", "expert")),
            P(("dp", "expert"), None),
            P(("dp", "expert"), None),
            P(("dp", "expert")),
            P(("dp", "expert"), None),
            P(("dp", "expert")),
            P(("dp", "expert")),
            P(("dp", "expert")),
            P(("dp", "expert"), None),
            P("expert", None, None),
            P("expert", None),
            P("expert", None, None),
            P("expert", None),
            P(("dp", "expert"), None, None),
        ),
        out_specs=(
            P(("dp", "expert"), None, None),
            P(("dp", "expert"), None, None),
            P(("dp", "expert")),
            P(("dp", "expert")),
            P(("dp", "expert"), None),
            P(("dp", "expert")),
            P(("dp", "expert"), None),
            P(("dp", "expert"), None),
            P(("dp", "expert")),
            P(("dp", "expert"), None),
            P(("dp", "expert")),
            P(("dp", "expert")),
            P(("dp", "expert")),
            P(("dp", "expert"), None),
            P("expert", "dp", None),
            P("expert", "dp"),
            P("expert", "dp", None),
            P("expert", "dp"),
        ),
        check_vma=False,
    )
```

profile of v0, /device:TPU:0, one launch (start us, length us, event | category | flops | bytes accessed | tf_op | source)
XLA Modules:
  0.0 1107.2 jit_solution(8980913062896648918)
XLA Ops:
  21.9 42.2 %all-reduce.17 = (bf16[768]{0:T(1024)(128)(2,1)S(1)}, bf16[768]{0:T(1024)(128)(2,1)S(1)}, bf16[768]{0:T(1024)(128)(2,1)S(1)}, bf16[768]{0:T(1024)(128)(2,1)S(1)}...) all-reduce(bf16[768]{0:T(1024)(128)(2,1)S(1)} %dynamic-update-slice, ...), channel_id=1, replica_groups=mesh['dp'=4,'expert'=8] {'dp','expert'}, use_global_device_ids=true, to_apply=%add.2 | all-reduce | flops 5376 | bytes 21504
  64.3 40.6 %all-gather = bf16[32,24,8]{1,2,0:T(8,128)(2,1)S(1)} all-gather(bf16[1,24,8]{1,2,0:T(8,128)(2,1)S(1)} %bitcast.295), channel_id=1, replica_groups=mesh['dp'=4,'expert'=8] {'dp','expert'}, dimensions={0}, use_global_device_ids=true | all-gather | bytes 12672 | tf_op jit(solution)/shard_map/all_gather | solution.py:65
  113.7 4.3 reshape.380
  118.0 3.9 mul.288
  121.9 7.1 mul.296
  131.2 3.4 add_convert_fusion.2
  134.6 3.4 add_convert_fusion.3
  138.0 41.8 %all-gather.10.cloned.1.call-done = bf16[768,768]{1,0:T(8,128)(2,1)} async-done(((bf16[24,768]{1,0:T(8,128)(2,1)}), bf16[768,768]{1,0:T(8,128)(2,1)}) %all-gather.10.cloned.1.call-update) | async-done | bytes 1179664 | tf_op jit(solution)/shard_map/all_gather | solution.py:58
  182.2 3.6 reshape.471
  185.8 3.9 copy.199
  189.7 3.5 reshape.469
  193.2 4.1 copy.200
  197.3 5.0 reshape.470
  202.3 4.8 copy.198
  207.2 2.9 multiply_reduce_fusion.1
  218.1 4.6 convert_element_type.198
  222.7 12.9 %all-gather.12.cloned.1.call-done = bf16[768,768]{1,0:T(8,128)(2,1)} async-done(((bf16[24,768]{1,0:T(8,128)(2,1)}), bf16[768,768]{1,0:T(8,128)(2,1)}) %all-gather.12.cloned.1.call-update) | async-done | bytes 1179664 | tf_op jit(solution)/shard_map/all_gather | solution.py:61
  235.6 3.0 fusion.77
  243.2 19.4 %scatter_custom_fusion.1 = bf16[1984,768]{1,0:T(8,128)(2,1)} fusion(s32[1576]{0:T(1024)S(1)} %fusion.67, f32[1576,768]{1,0:T(8,128)} %mul.296, f32[1576]{0:T(1024)S(1)} %mul.294, bf16[]{:T(256)} %constant.46.clone.1), kind=kCustom, calls=%fused_computation.85 | custom fusion | flops 2420736 | bytes 7897090 | tf_op jit(solution)/shard_map/scatter | solution.py:163
  262.7 4.6 all-to-all-start.2
  270.0 5.1 reshape.431
  275.2 12.8 %scatter_custom_fusion = bf16[1984,768]{1,0:T(8,128)(2,1)} fusion(s32[1576]{0:T(1024)S(1)} %fusion.67, bf16[1576,768]{1,0:T(8,128)(2,1)S(1)} %reshape.431, bf16[]{:T(256)} %constant.46.clone.1), kind=kCustom, calls=%fused_computation.97 | custom fusion | bytes 3047426 | tf_op jit(solution)/shard_map/scatter | solution.py:130
  287.9 16.2 %all-to-all-done.2 = bf16[8,248,768]{2,1,0:T(8,128)(2,1)} async-done(((bf16[8,248,768]{2,1,0:T(8,128)(2,1)}), bf16[8,248,768]{2,1,0:T(8,128)(2,1)}, u32[]{:S(2)}, u32[]{:S(2)}) %all-to-all-start.2) | async-done | bytes 3047456 | tf_op jit(solution)/shard_map/all_to_all | solution.py:165
  304.2 3.6 all-to-all-start
  311.2 33.4 %all-to-all-done = bf16[8,248,768]{2,1,0:T(8,128)(2,1)S(1)} async-done(((bf16[8,248,768]{2,1,0:T(8,128)(2,1)}), bf16[8,248,768]{2,1,0:T(8,128)(2,1)S(1)}, u32[]{:S(2)}, u32[]{:S(2)}) %all-to-all-start) | async-done | bytes 3047456 | tf_op jit(solution)/shard_map/all_to_all | solution.py:133
  344.6 16.3 %fusion.36 = f32[8,248,3072]{2,1,0:T(8,128)} fusion(bf16[8,248,768]{2,1,0:T(8,128)(2,1)S(1)} %all-to-all-done, bf16[1,768,3072]{2,1,0:T(8,128)(2,1)} %param.33), kind=kOutput, calls=%fused_computation.59 | convolution fusion | flops 9361686528 | bytes 32145408 | tf_op jit(solution)/shard_map/secd,edf->secf/dot_general | solution.py:136
  360.8 67.3 %fusion.79 = (bf16[3072]{0:T(1024)(128)(2,1)S(1)}, bf16[8,1,248,3072]{3,2,0,1:T(8,128)(2,1)}) fusion(bf16[8,248,768]{2,1,0:T(8,128)(2,1)} %all-to-all-done.2, bf16[1,3072,768]{2,1,0:T(8,128)(2,1)} %param.35, f32[3072]{0:T(1024)S(1)} %bitcast.292, f32[8,248,3072]{2,1,0:T(8,128)} %fusion.36), kind=kOutput, calls=%fused_computation.148 | convolution fusion | flops 9812702208 | bytes 44353536 | tf_op jit(solution)/shard_map/secd,efd->secf/dot_general | solution.py:172
  429.6 63.7 %fusion.38 = bf16[1,3072,768]{2,1,0:T(8,128)(2,1)} fusion(bf16[8,248,768]{2,1,0:T(8,128)(2,1)} %all-to-all-done.2, f32[8,248,3072]{2,1,0:T(8,128)} %fusion.36, f32[3072]{0:T(1024)S(1)} %bitcast.293), kind=kOutput, calls=%fused_computation.61 | convolution fusion | flops 9766305792 | bytes 32157696 | tf_op jit(solution)/shard_map/secf,secd->efd/dot_general | solution.py:168
  493.5 14.5 %fusion.39 = bf16[1,768,3072]{2,1,0:T(8,128)(2,1)} fusion(bf16[8,248,768]{2,1,0:T(8,128)(2,1)S(1)} %copy-done.19, bf16[8,1,248,3072]{3,2,0,1:T(8,128)(2,1)} %get-tuple-element.173), kind=kOutput, calls=%fused_computation.62 | convolution fusion | flops 9364045824 | bytes 19955712 | tf_op jit(solution)/shard_map/secd,secf->edf/dot_general | solution.py:180
  508.0 65.8 %fusion.42 = bf16[8,248,768]{2,1,0:T(8,128)(2,1)} fusion(f32[768]{0:T(1024)S(1)} %convert_reduce_fusion.4, bf16[1,3072,768]{2,1,0:T(8,128)(2,1)} %param.35, f32[8,248,3072]{2,1,0:T(8,128)} %fusion.36, f32[3072]{0:T(1024)S(1)} %bitcast.294), kind=kOutput, calls=%fused_computation.69 | convolution fusion | flops 9766993920 | bytes 32160768 | tf_op jit(solution)/shard_map/secf,efd->secd/dot_general | solution.py:141
  573.8 3.7 all-to-all-start.1
  577.5 15.1 %fusion.45 = bf16[8,248,768]{2,1,0:T(8,128)(2,1)} fusion(bf16[1,768,3072]{2,1,0:T(8,128)(2,1)} %param.33, bf16[8,1,248,3072]{3,2,0,1:T(8,128)(2,1)} %get-tuple-element.173), kind=kOutput, calls=%fused_computation.89 | convolution fusion | flops 9363210240 | bytes 19955712 | tf_op jit(solution)/shard_map/secf,edf->secd/dot_general | solution.py:184
  592.6 21.6 %all-to-all-done.1 = bf16[8,248,768]{2,1,0:T(8,128)(2,1)S(1)} async-done(((bf16[8,248,768]{2,1,0:T(8,128)(2,1)}), bf16[8,248,768]{2,1,0:T(8,128)(2,1)S(1)}, u32[]{:S(2)}, u32[]{:S(2)}) %all-to-all-start.1) | async-done | bytes 3047456 | tf_op jit(solution)/shard_map/all_to_all | solution.py:150
  615.9 3.7 all-to-all-start.3
  619.6 9.7 gather_fusion
  629.4 6.5 reshape.407
  635.8 13.9 %multiply_reduce_fusion.2 = (f32[788,2]{1,0:T(8,128)}, f32[788,768]{1,0:T(8,128)}) fusion(f32[788,2,768]{2,1,0:T(2,128)} %reshape.407, f32[788,768]{1,0:T(8,128)} %copy-done.2, f32[788,2]{1,0:T(8,128)S(1)} %copy-done.17), kind=kLoop, calls=%fused_computation.53 | loop fusion | flops 4234712 | bytes 9695552 | tf_op jit(solution)/shard_map/reduce_sum | solution.py:160
  650.9 5.4 all-to-all-done.3
  656.3 6.2 gather_fusion.1
  662.5 6.6 reshape.410
  669.2 9.7 reduce_sum.320
  679.1 3.7 multiply_reduce_fusion.4
  697.1 3.8 convolution_convert_fusion.2
  701.0 4.8 reshape.472
  705.8 4.9 copy.213
  710.7 6.6 convert_reduce_fusion
  719.6 4.2 reshape.402
  723.9 4.6 fusion.84
  728.9 11.1 %multiply_reduce_fusion = (f32[4,12,197]{2,1,0:T(8,128)S(1)}, f32[4,12,197,197]{2,3,1,0:T(8,128)}) fusion(f32[4,12,197,197]{2,3,1,0:T(8,128)} %copy-done, f32[4,12,197]{2,1,0:T(8,128)S(1)} %copy-done.21, bf16[4,197,12,64]{1,3,2,0:T(8,128)(2,1)} %copy.213, bf16[4,197,12,64]{1,3,2,0:T(8,128)(2,1)} %copy-done.12), kind=kOutput, calls=%fused_computation.43 | convolution fusion | flops 245884368 | bytes 17399040 | tf_op jit(solution)/shard_map/bqhd,bkhd->bhqk/dot_general | solution.py:259
  740.1 12.1 %multiply_convert_fusion = bf16[4,12,197,197]{2,3,1,0:T(8,128)(2,1)} fusion(f32[4,12,197,197]{2,3,1,0:T(8,128)} %get-tuple-element.166, f32[4,12,197,197]{2,3,1,0:T(8,128)} %copy-done, f32[4,12,197]{2,1,0:T(8,128)S(1)} %get-tuple-element.165, f32[4,12,197]{2,1,0:T(8,128)S(1)} %copy-done.21), kind=kLoop, calls=%fused_computation.42 | loop fusion | flops 9314160 | bytes 18703968 | tf_op jit(solution)/shard_map/convert_element_type | solution.py:265
  752.1 4.6 fusion.58
  759.1 4.2 reshape.401
  763.3 4.6 fusion.83
  768.1 4.1 convert_reduce_fusion.1
  774.5 4.2 reshape.400
  778.7 4.6 fusion.82
  793.9 3.2 fusion.81
  799.6 3.6 multiply_reduce_fusion.5
  803.2 39.4 %all-reduce.16 = (f32[768]{0:T(1024)S(1)}, f32[768]{0:T(1024)S(1)}, f32[768]{0:T(1024)S(1)}, f32[768]{0:T(1024)S(1)}, f32[768]{0:T(1024)S(1)}, /*index=5*/f32[76...) all-reduce(f32[768]{0:T(1024)S(1)} %get-tuple-element.128, ...), channel_id=2, replica_groups=mesh['dp'=4,'expert'=8] {'dp','expert'}, use_global_device_ids=true, to_apply=%region_25.26.clone | all-reduce | flops 11520 | bytes 92160
  846.7 3.3 fusion.75
  859.9 3.0 convert_element_type.233
  862.9 28.7 %reduce-scatter.18.cloned.1.call-done = f32[24,768]{1,0:T(8,128)} async-done(((f32[768,768]{1,0:T(8,128)}), f32[24,768]{1,0:T(8,128)}) %reduce-scatter.18.cloned.1.call-update) | async-done | bytes 73744 | tf_op jit(solution)/shard_map/reduce_scatter | solution.py:308
  891.6 104.7 %reduce-scatter.16.cloned.1.call-done = f32[24,768]{1,0:T(8,128)} async-done(((f32[768,768]{1,0:T(8,128)}), f32[24,768]{1,0:T(8,128)}) %reduce-scatter.16.cloned.1.call-update) | async-done | bytes 73744 | tf_op jit(solution)/shard_map/reduce_scatter | solution.py:307
  996.3 103.8 %reduce-scatter.14.cloned.1.call-done = f32[24,768]{1,0:T(8,128)} async-done(((f32[768,768]{1,0:T(8,128)}), f32[24,768]{1,0:T(8,128)}) %reduce-scatter.14.cloned.1.call-update) | async-done | bytes 73744 | tf_op jit(solution)/shard_map/reduce_scatter | solution.py:305
  (294 shorter events, 99.8 us)
Async XLA Ops:
  7.2 13.1 %copy-start.67 = (bf16[24]{0:T(256)(128)(2,1)S(1)}, bf16[24]{0:T(256)(128)(2,1)}, u32[]{:S(2)}) copy-start(bf16[24]{0:T(256)(128)(2,1)} %param.31) | copy-start | bytes 148
  7.2 13.3 %copy-start.68 = (bf16[24]{0:T(256)(128)(2,1)S(1)}, bf16[24]{0:T(256)(128)(2,1)}, u32[]{:S(2)}) copy-start(bf16[24]{0:T(256)(128)(2,1)} %param.29) | copy-start | bytes 148
  7.2 13.5 %copy-start.69 = (bf16[24]{0:T(256)(128)(2,1)S(1)}, bf16[24]{0:T(256)(128)(2,1)}, u32[]{:S(2)}) copy-start(bf16[24]{0:T(256)(128)(2,1)} %param.24) | copy-start | bytes 148
  7.2 13.7 %copy-start.70 = (bf16[24]{0:T(256)(128)(2,1)S(1)}, bf16[24]{0:T(256)(128)(2,1)}, u32[]{:S(2)}) copy-start(bf16[24]{0:T(256)(128)(2,1)} %param.27) | copy-start | bytes 148
  7.2 14.0 %copy-start.71 = (bf16[24]{0:T(256)(128)(2,1)S(1)}, bf16[24]{0:T(256)(128)(2,1)}, u32[]{:S(2)}) copy-start(bf16[24]{0:T(256)(128)(2,1)} %param.21) | copy-start | bytes 148
  7.2 14.2 %copy-start.72 = (bf16[24]{0:T(256)(128)(2,1)S(1)}, bf16[24]{0:T(256)(128)(2,1)}, u32[]{:S(2)}) copy-start(bf16[24]{0:T(256)(128)(2,1)} %param.22) | copy-start | bytes 148
  7.3 14.4 %copy-start.73 = (bf16[24]{0:T(256)(128)(2,1)S(1)}, bf16[24]{0:T(256)(128)(2,1)}, u32[]{:S(2)}) copy-start(bf16[24]{0:T(256)(128)(2,1)} %param.30) | copy-start | bytes 148
  7.3 57.0 %copy-start.65 = (bf16[24,8]{0,1:T(8,128)(2,1)S(1)}, bf16[24,8]{0,1:T(8,128)(2,1)}, u32[]{:S(2)}) copy-start(bf16[24,8]{0,1:T(8,128)(2,1)} %param.32) | copy-start | bytes 1156
  7.3 123.9 %all-gather.8.cloned.1.call-start = ((), (), s32[]{:S(2)}) async-start(), calls=%async_computation.13 | async-start | bytes 1216512 | tf_op jit(solution)/shard_map/all_gather | solution.py:56
  8.0 126.6 %all-gather.6.cloned.1.call-start = ((), (), s32[]{:S(2)}) async-start(), calls=%async_computation.12 | async-start | bytes 1216512 | tf_op jit(solution)/shard_map/all_gather | solution.py:59
  8.8 171.0 %all-gather.10.cloned.1.call-start = ((), (), s32[]{:S(2)}) async-start(), calls=%async_computation.14 | async-start | bytes 1216512 | tf_op jit(solution)/shard_map/all_gather | solution.py:58
  9.5 226.1 %all-gather.12.cloned.1.call-start = ((), (), s32[]{:S(2)}) async-start(), calls=%async_computation.15 | async-start | bytes 1216512 | tf_op jit(solution)/shard_map/all_gather | solution.py:61
  10.8 99.3 %copy-start.28 = (bf16[4,197,768]{2,0,1:T(4,128)(2,1)S(1)}, bf16[4,197,768]{2,0,1:T(4,128)(2,1)}, u32[]{:S(2)}) copy-start(bf16[4,197,768]{2,0,1:T(4,128)(2,1)} %param.37) | copy-start | bytes 3631108
  64.1 64.9 %copy-start.58 = (f32[768]{0:T(1024)}, f32[768]{0:T(1024)S(1)}, u32[]{:S(2)}) copy-start(f32[768]{0:T(1024)S(1)} %convert_element_type.188) | copy-start | bytes 9220
  64.1 64.9 %copy-start.36 = (f32[768]{0:T(1024)}, f32[768]{0:T(1024)S(1)}, u32[]{:S(2)}) copy-start(f32[768]{0:T(1024)S(1)} %convert_element_type.187) | copy-start | bytes 9220
  64.1 175.8 %copy-start.46 = (f32[768]{0:T(1024)}, f32[768]{0:T(1024)S(1)}, u32[]{:S(2)}) copy-start(f32[768]{0:T(1024)S(1)} %convert_element_type.200) | copy-start | bytes 9220
  64.3 177.3 %copy-start.50 = (s32[788,2]{0,1:T(2,128)}, s32[788,2]{0,1:T(2,128)S(1)}, u32[]{:S(2)}) copy-start(s32[788,2]{0,1:T(2,128)S(1)} %eq.31) | copy-start | bytes 18916
  105.0 136.0 %copy-start.34 = (bf16[768,8]{0,1:T(8,128)(2,1)}, bf16[768,8]{0,1:T(8,128)(2,1)S(1)}, u32[]{:S(2)}) copy-start(bf16[768,8]{0,1:T(8,128)(2,1)S(1)} %reshape.458) | copy-start | bytes 36868
  105.1 23.9 %copy-start.42 = (f32[788]{0:T(1024)}, f32[788]{0:T(1024)S(1)}, u32[]{:S(2)}) copy-start(f32[788]{0:T(1024)S(1)} %div.51) | copy-start | bytes 9460
  105.9 23.1 %copy-start.44 = (f32[788]{0:T(1024)}, f32[788]{0:T(1024)S(1)}, u32[]{:S(2)}) copy-start(f32[788]{0:T(1024)S(1)} %rsqrt.25) | copy-start | bytes 9460
  113.7 8.2 copy-start.2
  129.0 146.1 %copy-start.60 = (s32[1576]{0:T(1024)}, s32[1576]{0:T(1024)S(1)}, u32[]{:S(2)}) copy-start(s32[1576]{0:T(1024)S(1)} %fusion.67) | copy-start | bytes 18916
  182.2 7.5 copy-start.26
  189.7 17.5 %copy-start.13 = (bf16[4,197,12,64]{1,3,2,0:T(8,128)(2,1)}, bf16[4,197,12,64]{1,3,2,0:T(8,128)(2,1)S(1)}, u32[]{:S(2)}) copy-start(bf16[4,197,12,64]{1,3,2,0:T(8,128)(2,1)S(1)} %copy.199) | copy-start | bytes 3631108
  197.3 14.9 %copy-start.12 = (bf16[4,197,12,64]{1,3,2,0:T(8,128)(2,1)}, bf16[4,197,12,64]{1,3,2,0:T(8,128)(2,1)S(1)}, u32[]{:S(2)}) copy-start(bf16[4,197,12,64]{1,3,2,0:T(8,128)(2,1)S(1)} %copy.200) | copy-start | bytes 3631108
  210.1 3.6 copy-start
  215.7 19.8 %copy-start.7 = (f32[788,768]{1,0:T(8,128)S(1)}, f32[788,768]{1,0:T(8,128)}, u32[]{:S(2)}) copy-start(f32[788,768]{1,0:T(8,128)} %reshape.380) | copy-start | bytes 7262212
  241.1 26.3 %copy-start.11 = (bf16[788,768]{1,0:T(8,128)(2,1)}, bf16[788,768]{1,0:T(8,128)(2,1)S(1)}, u32[]{:S(2)}) copy-start(bf16[788,768]{1,0:T(8,128)(2,1)S(1)} %add_convert_fusion.1) | copy-start | bytes 3631108
  243.0 19.7 %copy-start.16 = (f32[788,2]{1,0:T(8,128)}, f32[788,2]{1,0:T(8,128)S(1)}, u32[]{:S(2)}) copy-start(f32[788,2]{1,0:T(8,128)S(1)} %copy.205) | copy-start | bytes 18916
  262.7 41.5 %all-to-all-start.2 = ((bf16[8,248,768]{2,1,0:T(8,128)(2,1)}), bf16[8,248,768]{2,1,0:T(8,128)(2,1)}, u32[]{:S(2)}, u32[]{:S(2)}) async-start(bf16[8,248,768]{2,1,0:T(8,128)(2,1)} %bitcast.287), calls=%async_computation.2 | async-start | bytes 6094848 | tf_op jit(solution)/shard_map/all_to_all | solution.py:165
  275.2 32.7 %copy-start.63 = (bf16[1,3072]{1,0:T(2,128)(2,1)S(1)}, bf16[1,3072]{1,0:T(2,128)(2,1)}, u32[]{:S(2)}) copy-start(bf16[1,3072]{1,0:T(2,128)(2,1)} %param.34) | copy-start | bytes 18436
  304.2 40.4 %all-to-all-start = ((bf16[8,248,768]{2,1,0:T(8,128)(2,1)}), bf16[8,248,768]{2,1,0:T(8,128)(2,1)S(1)}, u32[]{:S(2)}, u32[]{:S(2)}) async-start(bf16[8,248,768]{2,1,0:T(8,128)(2,1)} %bitcast.4), calls=%async_computation | async-start | bytes 6094848 | tf_op jit(solution)/shard_map/all_to_all | solution.py:133
  307.8 475.5 %reduce-scatter.28.cloned.1.call-start = ((), (), s32[]{:S(2)}) async-start(), calls=%async_computation.23 | async-start | bytes 245760
  311.1 473.7 %reduce-scatter.26.cloned.1.call-start = ((), (), s32[]{:S(2)}) async-start(), calls=%async_computation.22 | async-start | bytes 983040
  344.6 16.3 %copy-start.18 = (bf16[8,248,768]{2,1,0:T(8,128)(2,1)}, bf16[8,248,768]{2,1,0:T(8,128)(2,1)S(1)}, u32[]{:S(2)}) copy-start(bf16[8,248,768]{2,1,0:T(8,128)(2,1)S(1)} %all-to-all-done) | copy-start | bytes 9142276
  429.5 427.5 %reduce-scatter.24.cloned.1.call-start = ((), (), s32[]{:S(2)}) async-start(), calls=%async_computation.21 | async-start | bytes 5898240 | tf_op jit(solution)/shard_map/reduce_scatter | solution.py:196
  429.6 63.8 %copy-start.64 = (bf16[1,768]{1,0:T(2,128)(2,1)S(1)}, bf16[1,768]{1,0:T(2,128)(2,1)}, u32[]{:S(2)}) copy-start(bf16[1,768]{1,0:T(2,128)(2,1)} %param.36) | copy-start | bytes 4612
  429.6 63.9 %copy-start.19 = (bf16[8,248,768]{2,1,0:T(8,128)(2,1)S(1)}, bf16[8,248,768]{2,1,0:T(8,128)(2,1)}, u32[]{:S(2)}) copy-start(bf16[8,248,768]{2,1,0:T(8,128)(2,1)} %copy-done.18) | copy-start | bytes 9142276
  493.4 366.5 %reduce-scatter.22.cloned.1.call-start = ((), (), s32[]{:S(2)}) async-start(), calls=%async_computation.20 | async-start | bytes 5898240 | tf_op jit(solution)/shard_map/reduce_scatter | solution.py:190
  573.8 40.4 %all-to-all-start.1 = ((bf16[8,248,768]{2,1,0:T(8,128)(2,1)}), bf16[8,248,768]{2,1,0:T(8,128)(2,1)S(1)}, u32[]{:S(2)}, u32[]{:S(2)}) async-start(bf16[8,248,768]{2,1,0:T(8,128)(2,1)} %fusion.42), calls=%async_computation.1 | async-start | bytes 6094848 | tf_op jit(solution)/shard_map/all_to_all | solution.py:150
  592.6 27.0 %copy-start.61 = (s32[1576]{0:T(1024)S(1)}, s32[1576]{0:T(1024)}, u32[]{:S(2)}) copy-start(s32[1576]{0:T(1024)} %copy-done.60) | copy-start | bytes 18916
  615.9 40.4 %all-to-all-start.3 = ((bf16[8,248,768]{2,1,0:T(8,128)(2,1)}), bf16[8,248,768]{2,1,0:T(8,128)(2,1)S(1)}, u32[]{:S(2)}, u32[]{:S(2)}) async-start(bf16[8,248,768]{2,1,0:T(8,128)(2,1)} %fusion.45), calls=%async_computation.3 | async-start | bytes 6094848 | tf_op jit(solution)/shard_map/all_to_all | solution.py:186
  619.6 243.4 %reduce-scatter.20.cloned.1.call-start = ((), (), s32[]{:S(2)}) async-start(), calls=%async_computation.19 | async-start | bytes 2433024 | tf_op jit(solution)/shard_map/reduce_scatter | solution.py:310
  629.4 6.5 copy-start.17
  669.1 9.8 copy-start.51
  669.1 9.8 copy-start.33
  669.1 9.8 copy-start.41
  669.1 9.8 copy-start.55
  669.1 9.9 copy-start.5
  669.1 9.9 copy-start.31
  669.1 9.9 copy-start.35
  669.2 9.9 copy-start.39
  669.2 9.9 copy-start.47
  669.2 9.9 copy-start.49
  678.9 3.9 copy-start.53
  678.9 3.9 copy-start.6
  678.9 3.9 copy-start.14
  682.9 3.6 copy-start.3
  690.6 201.0 %reduce-scatter.18.cloned.1.call-start = ((), (), s32[]{:S(2)}) async-start(), calls=%async_computation.18 | async-start | bytes 2433024 | tf_op jit(solution)/shard_map/reduce_scatter | solution.py:308
  701.0 9.7 copy-start.21
  728.5 267.9 %reduce-scatter.16.cloned.1.call-start = ((), (), s32[]{:S(2)}) async-start(), calls=%async_computation.17 | async-start | bytes 2433024 | tf_op jit(solution)/shard_map/reduce_scatter | solution.py:307
  767.9 332.3 %reduce-scatter.14.cloned.1.call-start = ((), (), s32[]{:S(2)}) async-start(), calls=%async_computation.16 | async-start | bytes 2433024 | tf_op jit(solution)/shard_map/reduce_scatter | solution.py:305
  799.6 47.1 %copy-start.57 = (f32[788]{0:T(1024)S(1)}, f32[788]{0:T(1024)}, u32[]{:S(2)}) copy-start(f32[788]{0:T(1024)} %copy-done.56) | copy-start | bytes 9460
  842.6 7.4 copy-start.10
  (26 other events, 47.9 us)
Sparse Core Ops, SparseCore 0:
  11.0 56.9 all-gather.7
  70.9 52.9 all-gather.5
  126.8 52.9 all-gather.9
  182.6 52.9 all-gather.11
  311.3 19.6 reduce-scatter.27
  429.7 21.3 reduce-scatter.25
  493.5 83.2 reduce-scatter.23
  579.3 85.7 reduce-scatter.21
  690.8 96.9 reduce-scatter.19
  793.5 98.0 reduce-scatter.17
  898.4 97.9 reduce-scatter.15
  1002.1 98.0 reduce-scatter.13
where the time goes:
time: 1110 us
  waiting for transfers between devices  371 us (33%)
  matrix products  321 us (29%)
  local copies, waits for them, and re-layouts  172 us (15%)
  blocking collectives  122 us (11%)
  other arithmetic  88.7 us (8%)
  starting transfers between devices  16.7 us (2%)
  between operations  15.7 us (1%)
    reduce_scatter x1, waiting for transfers between devices, per_device(): lax.psum_scatter(grad_w_key, ('dp', 'expert'), scatter_dimension=0, tiled...  105 us
    reduce_scatter x1, waiting for transfers between devices, per_device(): lax.psum_scatter(grad_w_query, ('dp', 'expert'), scatter_dimension=0, til...  104 us
    unnamed x2, blocking collectives  81.6 us
    dot_general x1, matrix products, per_device(): jnp.einsum('secd,efd->secf', result_grad, w_down, preferred_element_type=...  67.3 us
    dot_general x1, matrix products, per_device(): jnp.einsum('secf,efd->secd', active_part, w_down, preferred_element_type=...  65.8 us
    dot_general x1, matrix products, per_device(): jnp.einsum('secf,secd->efd', active_four, result_grad, preferred_element_...  63.7 us
    all_gather x1, waiting for transfers between devices, per_device(): lax.all_gather(w_key, ('dp', 'expert'), axis=0, tiled=True)  41.8 us
    all_gather x1, blocking collectives, per_device(): lax.all_gather(w_router, ('dp', 'expert'), axis=0, tiled=True)  40.6 us
  transfers between devices with their start and end apart: 16, of which 9 were waited for; matrix products, arithmetic and copies ran while one was open for 49% of the time, Pallas kernels for 0%

commit v1 on v0

v1 whole, which is shorter than its diff:
```python
import functools

import jax
import jax.numpy as jnp
from jax import lax
from jax.experimental import pallas as pl
from jax.experimental.pallas import tpu as pltpu
from jax.sharding import PartitionSpec as P

HEADS = 12
HEAD_DIM = 64
PAIR = 2 * HEAD_DIM
EPSILON = 1e-06
SCALE = HEAD_DIM**-0.5
HIGHEST = lax.Precision.HIGHEST
VMEM_LIMIT = 60 * 1024 * 1024
BF16 = jnp.bfloat16
F32 = jnp.float32


def round_up(value, unit):
    return -(-value // unit) * unit


def dot(left, right):
    return jnp.dot(left, right, preferred_element_type=F32)


def dot_nt(left, right):
    return lax.dot_general(left, right, (((1,), (1,)), ((), ())), preferred_element_type=F32)


def dot_tn(left, right):
    return lax.dot_general(left, right, (((0,), (0,)), ((), ())), preferred_element_type=F32)


def params(grid_dims=1):
    return pltpu.CompilerParams(
        vmem_limit_bytes=VMEM_LIMIT, dimension_semantics=("arbitrary",) * grid_dims
    )


def whole(shape):
    zeros = (0,) * len(shape)
    return pl.BlockSpec(shape, lambda *_: zeros, pipeline_mode=pl.Buffered(1))


def per_image(*shape):
    zeros = (0,) * len(shape)
    return pl.BlockSpec((1,) + shape, lambda i: (i,) + zeros)


def norm_parts(values):
    center = values - jnp.mean(values, axis=-1, keepdims=True)
    inverse = lax.rsqrt(jnp.mean(center * center, axis=-1, keepdims=True) + EPSILON)
    return center * inverse, inverse


def norm_pull(unit, inverse, gain, grad):
    scaled = grad * gain
    return (
        scaled
        - jnp.mean(scaled, axis=-1, keepdims=True)
        - unit * jnp.mean(scaled * unit, axis=-1, keepdims=True)
    ) * inverse


def stack_heads(pair):
    low_half = lax.broadcasted_iota(jnp.int32, pair.shape, 1) < HEAD_DIM
    zero = jnp.zeros_like(pair)
    return jnp.concatenate(
        [jnp.where(low_half, pair, zero), jnp.where(low_half, zero, pair)], axis=0
    )


def merge_heads(stacked):
    rows = stacked.shape[0] // 2
    low_half = lax.broadcasted_iota(jnp.int32, (rows, PAIR), 1) < HEAD_DIM
    return jnp.where(low_half, stacked[:rows], stacked[rows:])


def pair_probs(query_stack, key_pair, seq_len):
    scores = dot_nt(query_stack, key_pair) * SCALE
    column = lax.broadcasted_iota(jnp.int32, scores.shape, 1)
    scores = jnp.where(column < seq_len, scores, -1e30)
    powers = jnp.exp(scores - jnp.max(scores, axis=1, keepdims=True))
    return powers * (1.0 / jnp.sum(powers, axis=1, keepdims=True))


def forward_kernel(
    seq_len,
    x_ref,
    wq_ref,
    wk_ref,
    wv_ref,
    wo_ref,
    vec_ref,
    router_ref,
    q_ref,
    k_ref,
    v_ref,
    att_ref,
    resid_ref,
    low_ref,
    gates_ref,
    gates_t_ref,
):
    x = x_ref[0].astype(F32)
    unit, _ = norm_parts(x)
    normed = (unit * vec_ref[0:1] + vec_ref[1:2]).astype(BF16)
    q_ref[0] = (dot(normed, wq_ref[...]) + vec_ref[2:3]).astype(BF16)
    k_ref[0] = dot(normed, wk_ref[...]).astype(BF16)
    v_ref[0] = (dot(normed, wv_ref[...]) + vec_ref[3:4]).astype(BF16)
    for j in range(HEADS // 2):
        cols = slice(j * PAIR, (j + 1) * PAIR)
        probs = pair_probs(stack_heads(q_ref[0, :, cols]), k_ref[0, :, cols], seq_len)
        mixed = merge_heads(dot(probs.astype(BF16), v_ref[0, :, cols]))
        att_ref[0, :, cols] = mixed.astype(BF16)
    resid = x + dot(att_ref[0], wo_ref[...]) + vec_ref[4:5]
    resid_ref[0] = resid
    unit_two, _ = norm_parts(resid)
    low = (unit_two * vec_ref[5:6] + vec_ref[6:7]).astype(BF16)
    low_ref[0] = low
    logits = dot(low, router_ref[...])
    powers = jnp.exp(logits - jnp.max(logits, axis=1, keepdims=True))
    gates = powers * (1.0 / jnp.sum(powers, axis=1, keepdims=True))
    gates_ref[0] = gates
    gates_t_ref[0] = gates.T


def run_forward(tokens, first, second, vectors, router, seq_len):
    images, rows, width = tokens.shape
    experts = router.shape[1]

    def column(j):
        return pl.BlockSpec((width, width), lambda i: (0, j), pipeline_mode=pl.Buffered(1))

    big = jax.ShapeDtypeStruct((images, rows, width), BF16)
    return pl.pallas_call(
        functools.partial(forward_kernel, seq_len),
        grid=(images,),
        in_specs=[
            per_image(rows, width),
            column(0),
            column(1),
            column(0),
            column(1),
            whole(vectors.shape),
            whole(router.shape),
        ],
        out_specs=[per_image(rows, width)] * 6
        + [per_image(rows, experts), per_image(experts, rows)],
        out_shape=[big, big, big, big, jax.ShapeDtypeStruct(big.shape, F32), big]
        + [
            jax.ShapeDtypeStruct((images, rows, experts), F32),
            jax.ShapeDtypeStruct((images, experts, rows), F32),
        ],
        compiler_params=params(),
        cost_estimate=pl.CostEstimate(
            flops=10 * images * rows * width * width, bytes_accessed=20_000_000, transcendentals=0
        ),
    )(tokens, first, first, second, second, vectors, router)


def dispatch_kernel(capacity, pos_ref, values_ref, *rest):
    gates_t_ref = rest[0] if len(rest) == 2 else None
    out_ref = rest[-1]
    expert = pl.program_id(0)
    images, rows, width = values_ref.shape
    slots = out_ref.shape[1]
    lanes = round_up(slots, 128)
    total = jnp.zeros((slots, width), F32)
    parts = jnp.zeros((8, lanes), F32)
    index = lax.broadcasted_iota(jnp.int32, (lanes, rows), 0)
    slot = jnp.where(index < slots, index + expert * slots, -2)
    for b in range(images):
        hit = (pos_ref[b, 0:1] == slot) | (pos_ref[b, 1:2] == slot)
        hit = jnp.where(hit, 1.0, 0.0).astype(BF16)
        total = total + dot(hit[:slots], values_ref[b])
        if gates_t_ref is not None:
            gate = jnp.broadcast_to(gates_t_ref[b, pl.ds(expert, 1)], (8, rows))
            high = gate.astype(BF16).astype(F32)
            middle = (gate - high).astype(BF16).astype(F32)
            part = lax.broadcasted_iota(jnp.int32, gate.shape, 0)
            split = jnp.where(
                part == 0,
                high,
                jnp.where(part == 1, middle, jnp.where(part == 2, gate - high - middle, 0.0)),
            )
            parts = parts + dot_nt(split.astype(BF16), hit)
    if gates_t_ref is not None:
        tail = jnp.concatenate([parts, jnp.zeros((8, width - lanes), F32)], axis=1)
        pieces = [total[:capacity], tail]
        if slots > capacity + 8:
            pieces.append(total[capacity + 8 :])
        total = jnp.concatenate(pieces, axis=0)
    out_ref[0] = total.astype(BF16)


def run_dispatch(pos_rows, values, capacity, slots, experts, gates_t=None):
    width = values.shape[2]
    operands = (pos_rows, values) + (() if gates_t is None else (gates_t,))
    return pl.pallas_call(
        functools.partial(dispatch_kernel, capacity),
        grid=(experts,),
        in_specs=[whole(o.shape) for o in operands],
        out_specs=pl.BlockSpec((1, slots, width), lambda i: (i, 0, 0)),
        out_shape=jax.ShapeDtypeStruct((experts, slots, width), BF16),
        compiler_params=params(),
        cost_estimate=pl.CostEstimate(
            flops=2 * experts * slots * values.shape[0] * values.shape[1] * width,
            bytes_accessed=6_000_000,
            transcendentals=0,
        ),
    )(*operands)


def gelu_parts(hidden):
    phi = 0.5 + 0.5 * lax.erf(hidden * (0.5**0.5))
    density = jnp.exp(hidden * hidden * -0.5) * 0.3989422804014327
    return hidden * phi, phi + hidden * density


def expert_forward_kernel(
    capacity,
    chunk,
    x_ref,
    cot_ref,
    up_ref,
    bias_up_ref,
    down_ref,
    bias_down_ref,
    result_ref,
    down_grad_ref,
    slope_ref,
    grad_ref,
    bias_grad_ref,
    total_ref,
    grad_t_ref,
    active_ref,
):
    step = pl.program_id(0)
    sources, slots, width = x_ref.shape
    rows = sources * slots
    lanes = round_up(slots, 128)

    @pl.when(step == 0)
    def _():
        bias_grad = jnp.zeros((1, width), F32)
        for s in range(sources):
            parts = x_ref[s, capacity : capacity + 8, :lanes].astype(F32)
            pick = jnp.broadcast_to(parts[0:1] + parts[1:2] + parts[2:3], (128, lanes)).T
            pick = jnp.concatenate([pick[:slots]] * (width // 128), axis=1)
            grad = (pick * cot_ref[s].astype(F32)).astype(BF16)
            grad_ref[s * slots : (s + 1) * slots, :] = grad
            bias_grad = bias_grad + jnp.sum(grad.astype(F32), axis=0, keepdims=True)
        bias_grad_ref[...] = bias_grad
        grad_t_ref[...] = grad_ref[...].T
        total_ref[...] = jnp.broadcast_to(bias_down_ref[...], total_ref.shape)

    x_flat = x_ref.reshape(rows, width)
    for r in range(rows // chunk):
        here = slice(r * chunk, (r + 1) * chunk)
        hidden = dot(x_flat[here, :], up_ref[...]) + bias_up_ref[...]
        active, slope = gelu_parts(hidden)
        active = active.astype(BF16)
        active_ref[here, :] = active
        slope_ref[here, :] = slope.astype(BF16)
        total_ref[here, :] += dot(active, down_ref[...])
    down_grad_ref[0] = dot(grad_t_ref[...], active_ref[...]).astype(BF16)

    @pl.when(step == pl.num_programs(0) - 1)
    def _():
        result_ref[...] = total_ref[...].astype(BF16)


def expert_backward_kernel(
    chunk,
    x_ref,
    grad_ref,
    slope_ref,
    up_ref,
    down_ref,
    entry_ref,
    up_grad_ref,
    bias_grad_ref,
    total_ref,
    x_t_ref,
    hidden_grad_ref,
):
    step = pl.program_id(0)
    rows = grad_ref.shape[0]

    @pl.when(step == 0)
    def _():
        x_t_ref[...] = x_ref[...].T
        total_ref[...] = jnp.zeros_like(total_ref)

    bias_grad = jnp.zeros(bias_grad_ref.shape, F32)
    for r in range(rows // chunk):
        here = slice(r * chunk, (r + 1) * chunk)
        active_grad = dot_nt(grad_ref[here, :], down_ref[...])
        hidden_grad = (active_grad * slope_ref[here, :].astype(F32)).astype(BF16)
        hidden_grad_ref[here, :] = hidden_grad
        bias_grad = bias_grad + jnp.sum(hidden_grad.astype(F32), axis=0, keepdims=True)
        total_ref[here, :] += dot_nt(hidden_grad, up_ref[...])
    bias_grad_ref[...] = bias_grad
    up_grad_ref[...] = dot(x_t_ref[...], hidden_grad_ref[...]).astype(BF16)

    @pl.when(step == pl.num_programs(0) - 1)
    def _():
        entry_ref[...] = total_ref[...].astype(BF16)


def run_experts_forward(x, cot, w_up, b_up, w_down, b_down, capacity, parts):
    sources, slots, width = x.shape
    rows = sources * slots
    units = w_up.shape[1]
    tile = units // parts
    chunk = 512 if rows % 512 == 0 else slots
    return pl.pallas_call(
        functools.partial(expert_forward_kernel, capacity, chunk),
        grid=(parts,),
        in_specs=[
            whole(x.shape),
            whole(cot.shape),
            pl.BlockSpec((width, tile), lambda i: (0, i)),
            pl.BlockSpec((1, tile), lambda i: (0, i)),
            pl.BlockSpec((tile, width), lambda i: (i, 0)),
            whole((1, width)),
        ],
        out_specs=[
            whole((rows, width)),
            pl.BlockSpec((1, width, tile), lambda i: (i, 0, 0)),
            pl.BlockSpec((rows, tile), lambda i: (0, i)),
            whole((rows, width)),
            whole((1, width)),
        ],
        out_shape=[
            jax.ShapeDtypeStruct((rows, width), BF16),
            jax.ShapeDtypeStruct((parts, width, tile), BF16),
            jax.ShapeDtypeStruct((rows, units), BF16),
            jax.ShapeDtypeStruct((rows, width), BF16),
            jax.ShapeDtypeStruct((1, width), F32),
        ],
        scratch_shapes=[
            pltpu.VMEM((rows, width), F32),
            pltpu.VMEM((width, rows), BF16),
            pltpu.VMEM((rows, tile), BF16),
        ],
        compiler_params=params(),
        cost_estimate=pl.CostEstimate(
            flops=6 * rows * width * units, bytes_accessed=40_000_000, transcendentals=rows * units
        ),
    )(x, cot, w_up, b_up, w_down, b_down)


def run_experts_backward(x, grad, slope, w_up, w_down, slots, parts):
    rows, width = x.shape
    units = w_up.shape[1]
    tile = units // parts
    chunk = 512 if rows % 512 == 0 else slots
    return pl.pallas_call(
        functools.partial(expert_backward_kernel, chunk),
        grid=(parts,),
        in_specs=[
            whole(x.shape),
            whole(grad.shape),
            pl.BlockSpec((rows, tile), lambda i: (0, i)),
            pl.BlockSpec((width, tile), lambda i: (0, i)),
            pl.BlockSpec((tile, width), lambda i: (i, 0)),
        ],
        out_specs=[
            whole((rows, width)),
            pl.BlockSpec((width, tile), lambda i: (0, i)),
            pl.BlockSpec((1, tile), lambda i: (0, i)),
        ],
        out_shape=[
            jax.ShapeDtypeStruct((rows, width), BF16),
            jax.ShapeDtypeStruct((width, units), BF16),
            jax.ShapeDtypeStruct((1, units), F32),
        ],
        scratch_shapes=[
            pltpu.VMEM((rows, width), F32),
            pltpu.VMEM((width, rows), BF16),
            pltpu.VMEM((rows, tile), BF16),
        ],
        compiler_params=params(),
        cost_estimate=pl.CostEstimate(
            flops=6 * rows * width * units, bytes_accessed=40_000_000, transcendentals=0
        ),
    )(x, grad, slope, w_up, w_down)


def combine_kernel(
    returned_ref, pos_ref, routes_ref, gates_ref, resid_ref, cot_ref, mixed_ref, logit_grad_ref
):
    slots = returned_ref.shape[0]
    rows, experts = gates_ref.shape[1:]
    gates = gates_ref[0]
    upstream = cot_ref[0].astype(F32)
    slot = lax.broadcasted_iota(jnp.int32, (rows, slots), 1)
    expert = lax.broadcasted_iota(jnp.int32, (rows, experts), 1)
    output = resid_ref[0]
    gate_grad = jnp.zeros((rows, experts), F32)
    for k in range(2):
        hit = jnp.where(pos_ref[0, :, k : k + 1] == slot, 1.0, 0.0).astype(BF16)
        picked = dot(hit, returned_ref[...])
        chosen = routes_ref[0, :, k : k + 1] == expert
        pick = jnp.sum(jnp.where(chosen, gates, 0.0), axis=1, keepdims=True)
        output = output + pick * picked
        pick_grad = jnp.sum(picked * upstream, axis=1, keepdims=True)
        gate_grad = gate_grad + jnp.where(chosen, pick_grad, 0.0)
    mixed_ref[0] = output.astype(BF16)
    logit_grad_ref[0] = gates * (gate_grad - jnp.sum(gates * gate_grad, axis=1, keepdims=True))


def run_combine(returned, pos_cols, routes_cols, gates, resid, cot):
    images, rows, width = resid.shape
    experts = gates.shape[2]
    return pl.pallas_call(
        combine_kernel,
        grid=(images,),
        in_specs=[
            whole(returned.shape),
            per_image(rows, 2),
            per_image(rows, 2),
            per_image(rows, experts),
            per_image(rows, width),
            per_image(rows, width),
        ],
        out_specs=[per_image(rows, width), per_image(rows, experts)],
        out_shape=[
            jax.ShapeDtypeStruct((images, rows, width), BF16),
            jax.ShapeDtypeStruct((images, rows, experts), F32),
        ],
        compiler_params=params(),
        cost_estimate=pl.CostEstimate(
            flops=4 * images * rows * width * returned.shape[0],
            bytes_accessed=10_000_000,
            transcendentals=0,
        ),
    )(returned, pos_cols, routes_cols, gates, resid, cot)


def backward_kernel(
    seq_len,
    entry_ref,
    pos_ref,
    logit_grad_ref,
    low_ref,
    resid_ref,
    cot_ref,
    x_ref,
    q_ref,
    k_ref,
    v_ref,
    att_ref,
    wq_ref,
    wk_ref,
    wv_ref,
    wo_ref,
    vec_ref,
    router_t_ref,
    x_grad_ref,
    first_ref,
    second_ref,
    small_ref,
    router_grad_ref,
    first_sum_ref,
    second_sum_ref,
    dq_ref,
    dk_ref,
    dv_ref,
):
    image = pl.program_id(0)
    slots = entry_ref.shape[0]
    rows, width = low_ref.shape[1:]

    @pl.when(image == 0)
    def _():
        first_sum_ref[...] = jnp.zeros_like(first_sum_ref)
        second_sum_ref[...] = jnp.zeros_like(second_sum_ref)
        small_ref[...] = jnp.zeros_like(small_ref)
        router_grad_ref[...] = jnp.zeros_like(router_grad_ref)

    def add_small(row, values):
        small_ref[row : row + 1, :] += jnp.sum(values, axis=0, keepdims=True)

    slot = lax.broadcasted_iota(jnp.int32, (rows, slots), 1)
    hit = (pos_ref[0, :, 0:1] == slot) | (pos_ref[0, :, 1:2] == slot)
    entry_sum = dot(jnp.where(hit, 1.0, 0.0).astype(BF16), entry_ref[...])
    logit_grad = logit_grad_ref[0]
    low_grad = entry_sum + jnp.dot(logit_grad, router_t_ref[...], precision=HIGHEST)
    router_grad_ref[...] += lax.dot_general(
        logit_grad,
        low_ref[0].astype(F32),
        (((0,), (0,)), ((), ())),
        precision=HIGHEST,
        preferred_element_type=F32,
    )
    unit, inverse = norm_parts(resid_ref[0])
    add_small(5, low_grad * unit)
    add_small(6, low_grad)
    resid_grad = cot_ref[0].astype(F32) + norm_pull(unit, inverse, vec_ref[5:6], low_grad)
    branch_grad = resid_grad.astype(BF16)
    add_small(4, branch_grad.astype(F32))
    second_sum_ref[:, width:] += dot_tn(att_ref[0], branch_grad)
    att_grad = dot_nt(branch_grad, wo_ref[...]).astype(BF16)
    for j in range(HEADS // 2):
        cols = slice(j * PAIR, (j + 1) * PAIR)
        query_stack = stack_heads(q_ref[0, :, cols])
        key_pair = k_ref[0, :, cols]
        probs = pair_probs(query_stack, key_pair, seq_len)
        grad_stack = stack_heads(att_grad[:, cols])
        dv_ref[:, cols] = dot_tn(probs.astype(BF16), grad_stack).astype(BF16)
        probs_grad = dot_nt(grad_stack, v_ref[0, :, cols])
        score_grad = probs * (
            probs_grad - jnp.sum(probs * probs_grad, axis=1, keepdims=True)
        )
        score_grad = score_grad.astype(BF16)
        dq_ref[:, cols] = (merge_heads(dot(score_grad, key_pair)) * SCALE).astype(BF16)
        dk_ref[:, cols] = (dot_tn(score_grad, query_stack) * SCALE).astype(BF16)
    dq, dk, dv = dq_ref[...], dk_ref[...], dv_ref[...]
    add_small(2, dq.astype(F32))
    add_small(3, dv.astype(F32))
    unit, inverse = norm_parts(x_ref[0].astype(F32))
    normed_t = (unit * vec_ref[0:1] + vec_ref[1:2]).astype(BF16).T
    first_sum_ref[:, :width] += dot(normed_t, dq)
    first_sum_ref[:, width:] += dot(normed_t, dk)
    second_sum_ref[:, :width] += dot(normed_t, dv)
    normed_grad = dot_nt(dq, wq_ref[...]) + dot_nt(dk, wk_ref[...]) + dot_nt(dv, wv_ref[...])
    add_small(0, normed_grad * unit)
    add_small(1, normed_grad)
    x_grad_ref[0] = resid_grad + norm_pull(unit, inverse, vec_ref[0:1], normed_grad)

    @pl.when(image == pl.num_programs(0) - 1)
    def _():
        first_ref[...] = first_sum_ref[...].astype(BF16)
        second_ref[...] = second_sum_ref[...].astype(BF16)


def run_backward(
    entry, pos_cols, logit_grad, low, resid, cot, tokens, saved, first, second, vectors, router_t,
    seq_len,
):
    images, rows, width = tokens.shape
    experts = router_t.shape[0]

    def column(j):
        return pl.BlockSpec((width, width), lambda i: (0, j), pipeline_mode=pl.Buffered(1))

    wide = (width, 2 * width)
    return pl.pallas_call(
        functools.partial(backward_kernel, seq_len),
        grid=(images,),
        in_specs=[
            whole(entry.shape),
            per_image(rows, 2),
            per_image(rows, experts),
        ]
        + [per_image(rows, width)] * 8
        + [column(0), column(1), column(0), column(1), whole(vectors.shape), whole(router_t.shape)],
        out_specs=[
            per_image(rows, width),
            whole(wide),
            whole(wide),
            whole((8, width)),
            whole((experts, width)),
        ],
        out_shape=[
            jax.ShapeDtypeStruct((images, rows, width), F32),
            jax.ShapeDtypeStruct(wide, BF16),
            jax.ShapeDtypeStruct(wide, BF16),
            jax.ShapeDtypeStruct((8, width), F32),
            jax.ShapeDtypeStruct((experts, width), F32),
        ],
        scratch_shapes=[pltpu.VMEM(wide, F32), pltpu.VMEM(wide, F32)]
        + [pltpu.VMEM((rows, width), BF16)] * 3,
        compiler_params=params(),
        cost_estimate=pl.CostEstimate(
            flops=24 * images * rows * width * width, bytes_accessed=30_000_000, transcendentals=0
        ),
    )(
        entry, pos_cols, logit_grad, low, resid, cot, tokens, *saved, first, first, second, second,
        vectors, router_t,
    )


def bits_of(size):
    return [1 << i for i in range(size.bit_length() - 1)]


def swap(values, axis, bit):
    return lax.ppermute(values, axis, [(i, i ^ bit) for i in range(lax.axis_size(axis))])


def my_bit(axis, bit):
    return (lax.axis_index(axis) // bit) % 2


def axis_order(reverse):
    expert_bits = bits_of(lax.axis_size("expert"))
    others = expert_bits[1:]
    if not reverse:
        others = others[::-1]
    return [("expert", bit) for bit in others] + [("expert", expert_bits[0])]


def natural_order():
    return [("dp", bit) for bit in bits_of(lax.axis_size("dp"))[::-1]] + [
        ("expert", bit) for bit in bits_of(lax.axis_size("expert"))[::-1]
    ]


def gather_rows(shard, reverse):
    rows, columns = shard.shape
    order = [("dp", bit) for bit in bits_of(lax.axis_size("dp"))] + axis_order(reverse)
    for axis, bit in order:
        other = swap(shard, axis, bit)
        mine_low = my_bit(axis, bit) == 0
        shard = jnp.stack(
            [jnp.where(mine_low, shard, other), jnp.where(mine_low, other, shard)]
        )
    dims = order[::-1]
    turn = [dims.index(pair) for pair in natural_order()]
    shard = shard.transpose(turn + [len(dims), len(dims) + 1])
    return shard.reshape(-1, columns)


def scatter_rows(total, reverse, axes=("dp", "expert")):
    columns = total.shape[-1]
    dims = [pair for pair in natural_order() if pair[0] in axes]
    total = total.reshape((2,) * len(dims) + (-1, columns))
    order = [("dp", bit) for bit in bits_of(lax.axis_size("dp"))] + axis_order(reverse)
    for pair in [p for p in order[::-1] if p[0] in axes]:
        place = dims.index(pair)
        mine = my_bit(*pair)
        sent = lax.dynamic_index_in_dim(total, 1 - mine, place, keepdims=False)
        kept = lax.dynamic_index_in_dim(total, mine, place, keepdims=False)
        total = (kept.astype(F32) + swap(sent, *pair).astype(F32)).astype(total.dtype)
        dims.pop(place)
    return total


def per_device(
    tokens,
    routes,
    gain_one,
    shift_one,
    w_query,
    b_query,
    w_key,
    w_value,
    b_value,
    w_out,
    b_out,
    gain_two,
    shift_two,
    w_router,
    w_up,
    b_up,
    w_down,
    b_down,
    cotangent,
):
    images, seq_len, width = tokens.shape
    token_rows = images * seq_len
    parts = lax.axis_size("dp")
    experts = w_up.shape[0] * lax.axis_size("expert")
    capacity = max((token_rows * 10 // (4 * experts) + 7) // 8 * 8, 8)
    slots = round_up(capacity + 8, 16)
    rows = round_up(seq_len, 16)
    pad = ((0, 0), (0, rows - seq_len), (0, 0))

    vectors = (gain_one, shift_one, b_query, b_value, b_out, gain_two, shift_two)
    spare = jnp.zeros((w_query.shape[0], 128 - len(vectors) - experts), BF16)
    small = jnp.concatenate([jnp.stack(vectors, axis=1), w_router, spare], axis=1)
    first = gather_rows(jnp.concatenate([w_query, w_key], axis=1), False)
    second = gather_rows(jnp.concatenate([w_value, w_out, small], axis=1), True)
    small = second[:, 2 * width :]
    vectors = jnp.pad(small[:, : len(vectors)].T.astype(F32), ((0, 8 - len(vectors)), (0, 0)))
    router = small[:, 7 : 7 + experts]
    router_t = router.T.astype(F32)

    flat_routes = routes.reshape(-1)
    table = (flat_routes[:, None] == jnp.arange(experts, dtype=jnp.int32)[None, :]).astype(
        jnp.int32
    )
    before = jnp.cumsum(table, axis=0) - table
    position = flat_routes * slots + jnp.sum(before * table, axis=1)
    pos_cols = jnp.pad(position.reshape(images, seq_len, 2), pad, constant_values=-1)
    routes_cols = jnp.pad(routes, pad, constant_values=-1)
    pos_rows = pos_cols.transpose(0, 2, 1)

    x = jnp.pad(tokens, pad)
    cot = jnp.pad(cotangent, pad)
    cot_sent = run_dispatch(pos_rows, cot, capacity, slots, experts)
    cot_here = lax.all_to_all(cot_sent, "expert", split_axis=0, concat_axis=0, tiled=True)

    query, key, value, attended, resid, low, gates, gates_t = run_forward(
        x, first, second, vectors, router, seq_len
    )
    low_sent = run_dispatch(pos_rows, low, capacity, slots, experts, gates_t)
    low_here = lax.all_to_all(low_sent, "expert", split_axis=0, concat_axis=0, tiled=True)

    up, down = w_up[0], w_down[0]
    result, down_grad, slope, result_grad, bias_down_grad = run_experts_forward(
        low_here, cot_here, up, b_up.astype(F32), down, b_down.astype(F32), capacity, parts
    )
    returned = lax.all_to_all(
        result.reshape(experts, slots, width), "expert", split_axis=0, concat_axis=0, tiled=True
    )
    down_shard = lax.psum_scatter(down_grad, "dp", scatter_dimension=0, tiled=True)
    entry, up_grad, bias_up_grad = run_experts_backward(
        low_here.reshape(experts * slots, width), result_grad, slope, up, down, slots, parts
    )
    entry_back = lax.all_to_all(
        entry.reshape(experts, slots, width), "expert", split_axis=0, concat_axis=0, tiled=True
    )
    up_shard = lax.psum_scatter(up_grad, "dp", scatter_dimension=0, tiled=True)
    mixed, logit_grad = run_combine(
        returned.reshape(experts * slots, width), pos_cols, routes_cols, gates, resid, cot
    )
    x_grad, first_grad, second_grad, small_grad, router_grad = run_backward(
        entry_back.reshape(experts * slots, width),
        pos_cols,
        logit_grad,
        low,
        resid,
        cot,
        x,
        (query, key, value, attended),
        first,
        second,
        vectors,
        router_t,
        seq_len,
    )
    narrow = jnp.concatenate([small_grad[:7], router_grad], axis=0).T
    narrow = jnp.pad(narrow, ((0, 0), (0, 128 - narrow.shape[1]))).astype(BF16)
    first_shard = scatter_rows(first_grad, False).astype(F32)
    second_shard = scatter_rows(jnp.concatenate([second_grad, narrow], axis=1), True).astype(F32)
    biases = jnp.concatenate(
        [bias_up_grad.reshape(parts, -1), bias_down_grad.reshape(parts, -1)], axis=1
    )
    biases = scatter_rows(biases, False, ("dp",)).reshape(1, -1)
    columns = second_shard[:, 2 * width :]
    tile = down_shard.shape[2]
    return (
        mixed[:, :seq_len],
        x_grad[:, :seq_len],
        columns[:, 0],
        columns[:, 1],
        first_shard[:, :width],
        columns[:, 2],
        first_shard[:, width:],
        second_shard[:, :width],
        columns[:, 3],
        second_shard[:, width : 2 * width],
        columns[:, 4],
        columns[:, 5],
        columns[:, 6],
        columns[:, 7 : 7 + experts],
        up_shard.astype(F32)[None],
        biases[:, :tile],
        down_shard.transpose(0, 2, 1).astype(F32),
        biases[:, tile:],
    )


def solution(mesh):
    both = ("dp", "expert")
    row, matrix, cube = P(both), P(both, None), P(both, None, None)
    return jax.shard_map(
        per_device,
        mesh=mesh,
        in_specs=(
            cube, cube, row, row, matrix, row, matrix, matrix, row, matrix, row, row, row, matrix,
            P("expert", None, None),
            P("expert", None),
            P("expert", None, None),
            P("expert", None),
            cube,
        ),
        out_specs=(
            cube, cube, row, row, matrix, row, matrix, matrix, row, matrix, row, row, row, matrix,
            P("expert", "dp", None),
            P("expert", "dp"),
            P("expert", "dp", None),
            P("expert", "dp"),
        ),
        check_vma=False,
    )
```

time: 1110 us -> 432 us (0.39)
  matrix products: 321 us -> 0 us
  waiting for transfers between devices: 371 us -> 134 us
  Pallas kernels: 0 us -> 171 us
  local copies, waits for them, and re-layouts: 172 us -> 40 us
  blocking collectives: 122 us -> 0 us
  other arithmetic: 88.7 us -> 25.1 us
  starting transfers between devices: 16.7 us -> 39.5 us
    dot_general x27 -> x0, matrix products: 321 us -> none  [the longest x1 67.3 us: per_device(): jnp.einsum('secd,efd->secf', result_grad, w_down, preferred_element_type=...]
    reduce_scatter x6 -> x2, waiting for transfers between devices: 237 us -> 0.01 us  [the longest x1 0.01 us: per_device(): lax.psum_scatter(down_grad, 'dp', scatter_dimension=0, tiled=True)]
    pallas_call x0 -> x7, Pallas kernels: none -> 171 us  [the longest x1 43.9 us: run_experts_forward(): pl.pallas_call(functools.partial(expert_forward_kernel, capacity, chunk),...]
    unnamed x2 -> x0, blocking collectives: 81.6 us -> none
    ppermute x0 -> x22, waiting for transfers between devices: none -> 72.2 us  [swap(): lax.ppermute(values, axis, [(i, i ^ bit) for i in range(lax.axis_size(axi...]
    reshape x17 -> x0, local copies, waits for them, and re-layouts: 64.9 us -> none  [the longest x2 9.84 us: per_device(): query = (matmul(normed_low, full_query) + full_bias_query.astype(jnp.floa...]
    all_gather x4 -> x0, waiting for transfers between devices: 54.6 us -> none  [the longest x1 41.8 us: per_device(): lax.all_gather(w_key, ('dp', 'expert'), axis=0, tiled=True)]
    all_gather x1 -> x0, blocking collectives: 40.6 us -> none  [per_device(): lax.all_gather(w_router, ('dp', 'expert'), axis=0, tiled=True)]
  transfers between devices with their start and end apart: 16 -> 28, of which waited for: 9 -> 17; matrix products, arithmetic and copies ran while one was open for 49% -> 14% of each run, Pallas kernels for 0% -> 30%
where the time goes in v1:
time: 432 us; the launch traced here: 425 us
  Pallas kernels  171 us (40%)
  waiting for transfers between devices  134 us (31%)
  local copies, waits for them, and re-layouts  40 us (9%)
  starting transfers between devices  39.5 us (9%)
  other arithmetic  25.1 us (6%)
  between operations  15 us (3%)
    ppermute x22, waiting for transfers between devices, swap(): lax.ppermute(values, axis, [(i, i ^ bit) for i in range(lax.axis_size(axi...  72.2 us
    pallas_call x1, Pallas kernels, run_experts_forward(): pl.pallas_call(functools.partial(expert_forward_kernel, capacity, chunk),...  43.9 us
    pallas_call x1, Pallas kernels, run_backward(): pl.pallas_call(functools.partial(backward_kernel, seq_len), grid=(images,...  43.7 us
    pallas_call x1, Pallas kernels, run_experts_backward(): pl.pallas_call(functools.partial(expert_backward_kernel, chunk), grid=(pa...  40.1 us
    all_to_all x1, waiting for transfers between devices, per_device(): lax.all_to_all(low_sent, 'expert', split_axis=0, concat_axis=0, tiled=True)  35 us
    all_to_all x1, waiting for transfers between devices, per_device(): lax.all_to_all(entry.reshape(experts, slots, width), 'expert', split_axis...  24.3 us
    ppermute x22, starting transfers between devices, swap(): lax.ppermute(values, axis, [(i, i ^ bit) for i in range(lax.axis_size(axi...  21.5 us
    pallas_call x1, Pallas kernels, run_forward(): pl.pallas_call(functools.partial(forward_kernel, seq_len), grid=(images,)...  18 us
  transfers between devices with their start and end apart: 28, of which 17 were waited for; matrix products, arithmetic and copies ran while one was open for 14% of the time, Pallas kernels for 30%

profile of v1, /device:TPU:0, one launch (start us, length us, event | category | flops | bytes accessed | tf_op | source)
XLA Modules:
  0.0 424.5 jit_solution(14821760998483569793)
XLA Ops:
  8.7 3.0 collective-permute-start
  17.8 0.9 concatenate.22
  19.5 0.9 copy.168
  20.9 2.3 reduce-window.6
  24.1 0.8 fusion.19
  25.8 1.2 pad.34.values_ref.cot_ref
  27.0 3.0 collective-permute-start.1
  30.2 10.9 %collective-permute-done.1 = bf16[2,24,1536]{2,1,0:T(8,128)(2,1)S(1)} collective-permute-done((bf16[2,24,1536]{2,1,0:T(8,128)(2,1)S(1)}, bf16[2,24,1536]{2,1,0:T(8,128)(2,1)S(1)}, u32[]{:S(2)}, u32[]{:S(2)}) %collective-permute-start.1) | collective-permute-done | bytes 147488 | tf_op jit(solution)/shard_map/ppermute | solution.py:595
  41.2 1.6 collective-permute-start.2
  43.4 1.6 collective-permute-start.7
  45.0 3.0 collective-permute-done.2
  48.1 1.6 collective-permute-start.3
  49.7 4.3 %collective-permute-done.7 = bf16[2,2,24,1664]{3,2,1,0:T(8,128)(2,1)S(1)} collective-permute-done((bf16[2,2,24,1664]{3,2,1,0:T(8,128)(2,1)S(1)}, bf16[2,2,24,1664]{3,2,1,0:T(8,128)(2,1)S(1)}, u32[]{:S(2)}, u32[]{:S(2)}) %collective-permute-start.7) | collective-permute-done | bytes 319520 | tf_op jit(solution)/shard_map/ppermute | solution.py:595
  54.1 1.6 collective-permute-start.8
  55.8 8.7 %collective-permute-done.3 = bf16[2,2,2,24,1536]{4,3,2,1,0:T(8,128)(2,1)S(1)} collective-permute-done((bf16[2,2,2,24,1536]{4,3,2,1,0:T(8,128)(2,1)S(1)}, bf16[2,2,2,24,1536]{4,3,2,1,0:T(8,128)(2,1)S(1)}, u32[]{:S(2)}, u32[]{:S(2)}) %collective-permute-start.3) | collective-permute-done | bytes 589856 | tf_op jit(solution)/shard_map/ppermute | solution.py:595
  64.6 1.1 pad_maximum_fusion.2
  66.5 1.2 pad_maximum_fusion.1
  67.7 7.3 %shard_map.324 = bf16[8,256,768]{2,1,0:T(8,128)(2,1)} custom-call(s32[4,2,208]{2,1,0:T(2,128)} %copy.187.pos_ref, bf16[4,208,768]{2,1,0:T(8,128)(2,1)} %pad.34.values_ref.cot_ref), custom_call_target="tpu_custom_call" | custom-call | flops 2617245696 | bytes 6000000 | tf_op jit(solution)/shard_map/pallas_call | solution.py:203
  74.9 4.4 %all-to-all-start.1 = ((bf16[8,256,768]{2,1,0:T(8,128)(2,1)}), bf16[8,256,768]{2,1,0:T(8,128)(2,1)}, u32[]{:S(2)}, u32[]{:S(2)}) async-start(bf16[8,256,768]{2,1,0:T(8,128)(2,1)} %shard_map.324), calls=%async_computation.1 | async-start | bytes 6291456 | tf_op jit(solution)/shard_map/all_to_all | solution.py:699
  79.4 1.4 copy.171
  80.8 1.1 pad.31.x_ref
  81.9 1.4 select_bitcast_fusion.3
  83.6 1.7 copy.172
  85.2 1.6 select_bitcast_fusion.1
  87.1 0.9 slice.104.router_ref
  89.4 18.0 %shard_map.322 = (bf16[4,208,768]{2,1,0:T(8,128)(2,1)}, bf16[4,208,768]{2,1,0:T(8,128)(2,1)}, bf16[4,208,768]{2,1,0:T(8,128)(2,1)}, bf16[4,208,768]{2,1,0:T(8,12...) custom-call(bf16[4,208,768]{2,1,0:T(8,128)(2,1)} %pad.31.x_ref, ...), custom_call_target="tpu_custom_call" | custom-call | flops 4907335680 | bytes 20000000 | tf_op jit(solution)/shard_map/pallas_call | solution.py:139
  107.3 7.7 %shard_map.323 = bf16[8,256,768]{2,1,0:T(8,128)(2,1)} custom-call(s32[4,2,208]{2,1,0:T(2,128)} %copy.187.pos_ref, bf16[4,208,768]{2,1,0:T(8,128)(2,1)} %get-tuple-element.41.values_ref.low_ref, f32[4,8,208]{2,1,0:T(8,128)} %get-tuple-element.42.rest_0_), custom_call_target="tpu_custom_call" | custom-call | flops 2617245696 | bytes 6000000 | tf_op jit(solution)/shard_map/pallas_call | solution.py:203
  115.0 2.3 all-to-all-done.1.cot_ref
  117.3 3.6 all-to-all-start
  121.2 1.3 convert_element_type.163.bias_down_ref
  122.4 1.3 convert_element_type.162.bias_up_ref
  123.8 35.0 %all-to-all-done.x_ref = bf16[8,256,768]{2,1,0:T(8,128)(2,1)S(1)} async-done(((bf16[8,256,768]{2,1,0:T(8,128)(2,1)}), bf16[8,256,768]{2,1,0:T(8,128)(2,1)S(1)}, u32[]{:S(2)}, u32[]{:S(2)}) %all-to-all-start) | async-done | bytes 3145760 | tf_op jit(solution)/shard_map/all_to_all | solution.py:705
  158.7 1.7 copy-done.2
  160.5 43.9 %shard_map.325 = (bf16[2048,768]{1,0:T(8,128)(2,1)}, bf16[4,768,768]{2,1,0:T(8,128)(2,1)}, bf16[2048,3072]{1,0:T(8,128)(2,1)}, bf16[2048,768]{1,0:T(8,128)(2,1)}, f32[1,768]{1,0:T(1,128)}) custom-call(bf16[8,256,768]{2,1,0:T(8,128)(2,1)} %copy-done.2, bf16[8,256,768]{2,1,0:T(8,128)(2,1)} %all-to-all-done.1.cot_ref, bf16[768,3072]{1,0:T(8,128)(2,1)} %bitcast.181, ...), custom_call_target="tpu_custom_call" | custom-call | flops 28991029248 | bytes 40000000 | tf_op jit(solution)/shard_map/pallas_call | solution.py:321
  204.4 4.9 %all-to-all-start.2 = ((bf16[8,256,768]{2,1,0:T(8,128)(2,1)}), bf16[8,256,768]{2,1,0:T(8,128)(2,1)}, u32[]{:S(2)}, u32[]{:S(2)}) async-start(bf16[8,256,768]{2,1,0:T(8,128)(2,1)} %bitcast.41), calls=%async_computation.2 | async-start | bytes 6291456 | tf_op jit(solution)/shard_map/all_to_all | solution.py:711
  209.3 40.1 %shard_map.327 = (bf16[2048,768]{1,0:T(8,128)(2,1)}, bf16[768,3072]{1,0:T(8,128)(2,1)}, f32[1,3072]{1,0:T(1,128)}) custom-call(bf16[2048,768]{1,0:T(8,128)(2,1)} %bitcast.165, bf16[2048,768]{1,0:T(8,128)(2,1)} %get-tuple-element.47.grad_ref, bf16[2048,3072]{1,0:T(8,128)(2,1)} %get-tuple-element.48.slope_ref, bf16[768,3072]{1,0:T(8,128)(2,1)} %bitcast.182, ...), custom_call_target="tpu_custom_call" | custom-call | flops 28991029248 | bytes 40000000 | tf_op jit(solution)/shard_map/pallas_call | solution.py:363
  249.5 4.6 %all-to-all-start.3 = ((bf16[8,256,768]{2,1,0:T(8,128)(2,1)}), bf16[8,256,768]{2,1,0:T(8,128)(2,1)}, u32[]{:S(2)}, u32[]{:S(2)}) async-start(bf16[8,256,768]{2,1,0:T(8,128)(2,1)} %bitcast.164), calls=%async_computation.3 | async-start | bytes 6291456 | tf_op jit(solution)/shard_map/all_to_all | solution.py:718
  257.3 10.4 %shard_map.326 = (bf16[4,208,768]{2,1,0:T(8,128)(2,1)}, f32[4,208,8]{2,1,0:T(8,128)}) custom-call(bf16[2048,768]{1,0:T(8,128)(2,1)} %bitcast.42.returned_ref, s32[4,208,2]{2,1,0:T(8,128)} %get-tuple-element.175.pos_ref, s32[4,208,2]{2,1,0:T(8,128)} %pad.35.routes_ref, f32[4,208,8]{2,1,0:T(8,128)} %get-tuple-element.44.gates_ref, ...), custom_call_target="tpu_custom_call" | custom-call | flops 5234491392 | bytes 10000000 | tf_op jit(solution)/shard_map/pallas_call | solution.py:421
  267.7 24.3 %all-to-all-done.3 = bf16[8,256,768]{2,1,0:T(8,128)(2,1)} async-done(((bf16[8,256,768]{2,1,0:T(8,128)(2,1)}), bf16[8,256,768]{2,1,0:T(8,128)(2,1)}, u32[]{:S(2)}, u32[]{:S(2)}) %all-to-all-start.3) | async-done | bytes 3145760 | tf_op jit(solution)/shard_map/all_to_all | solution.py:718
  291.9 43.7 %shard_map.328 = (f32[4,208,768]{2,1,0:T(8,128)}, bf16[768,1536]{1,0:T(8,128)(2,1)}, bf16[768,1536]{1,0:T(8,128)(2,1)}, f32[8,768]{1,0:T(8,128)}, f32[8,768]{1,0:T(8,128)}) custom-call(bf16[2048,768]{1,0:T(8,128)(2,1)} %bitcast.45.entry_ref, s32[4,208,2]{2,1,0:T(8,128)} %get-tuple-element.175.pos_ref, f32[4,208,8]{2,1,0:T(8,128)} %get-tuple-element.50.logit_grad_ref, ...), custom_call_target="tpu_custom_call" | custom-call | flops 11777605632 | bytes 30000000 | tf_op jit(solution)/shard_map/pallas_call | solution.py:554
  337.2 2.9 constant_dynamic-slice_fusion.3
  340.0 1.1 copy.210
  341.3 1.9 fusion.1
  343.2 1.1 dynamic-slice_bitcast_fusion
  344.9 3.2 collective-permute-start.21
  348.1 4.2 collective-permute-done.21
  353.4 1.5 slice.84
  355.0 1.5 copy.195
  356.7 2.4 copy.196
  359.0 1.6 fusion.3
  360.8 1.6 fusion.2
  362.5 13.6 %collective-permute-done.16 = bf16[2,2,2,24,1536]{4,3,1,0,2:T(8,128)(2,1)S(1)} collective-permute-done((bf16[2,2,2,24,1536]{4,3,1,0,2:T(8,128)(2,1)S(1)}, bf16[2,2,2,24,1536]{4,3,1,0,2:T(8,128)(2,1)S(1)}, u32[]{:S(2)}, u32[]{:S(2)}) %collective-permute-start.16) | collective-permute-done | bytes 589856 | tf_op jit(solution)/shard_map/ppermute | solution.py:595
  376.4 3.1 collective-permute-done.11
  379.6 5.6 %collective-permute-done.17 = bf16[2,2,24,1536]{3,2,1,0:T(8,128)(2,1)S(1)} collective-permute-done((bf16[2,2,24,1536]{3,2,1,0:T(8,128)(2,1)S(1)}, bf16[2,2,24,1536]{3,2,1,0:T(8,128)(2,1)S(1)}, u32[]{:S(2)}, u32[]{:S(2)}) %collective-permute-start.17) | collective-permute-done | bytes 294944 | tf_op jit(solution)/shard_map/ppermute | solution.py:595
  386.0 1.5 collective-permute-start.12
  387.5 6.8 %collective-permute-done.18 = bf16[2,24,1536]{2,1,0:T(8,128)(2,1)S(1)} collective-permute-done((bf16[2,24,1536]{2,1,0:T(8,128)(2,1)S(1)}, bf16[2,24,1536]{2,1,0:T(8,128)(2,1)S(1)}, u32[]{:S(2)}, u32[]{:S(2)}) %collective-permute-start.18) | collective-permute-done | bytes 147488 | tf_op jit(solution)/shard_map/ppermute | solution.py:595
  394.6 2.4 collective-permute-start.13
  397.0 2.5 collective-permute-done.19
  399.5 4.8 %collective-permute-done.13 = bf16[2,24,1664]{2,1,0:T(8,128)(2,1)S(1)} collective-permute-done((bf16[2,24,1664]{2,1,0:T(8,128)(2,1)S(1)}, bf16[2,24,1664]{2,1,0:T(8,128)(2,1)S(1)}, u32[]{:S(2)}, u32[]{:S(2)}) %collective-permute-start.13) | collective-permute-done | bytes 159776 | tf_op jit(solution)/shard_map/ppermute | solution.py:595
  405.4 3.5 collective-permute-done.14
  409.6 0.8 slice_reduce_fusion.1
  411.1 1.4 convert_bitcast_fusion
  412.6 2.0 copy.198
  414.5 2.9 bitcast_convert_fusion
  (131 shorter events, 25.4 us)
Async XLA Ops:
  8.7 18.3 %collective-permute-start = (bf16[24,1536]{1,0:T(8,128)(2,1)S(1)}, bf16[24,1536]{1,0:T(8,128)(2,1)S(1)}, u32[]{:S(2)}, u32[]{:S(2)}) collective-permute-start(bf16[24,1536]{1,0:T(8,128)(2,1)S(1)} %constant_dynamic-update-slice_fusion), channel_id=1, source_target_pairs={{0,8},{8,0},{16,24},{24,16},{1,9},{9,1},{17,25},{25,17},{2,10},{10... | collective-permute-start | bytes 221192 | tf_op jit(solution)/shard_map/ppermute | solution.py:595
  18.6 11.4 %collective-permute-start.5 = (bf16[24,1664]{1,0:T(8,128)(2,1)S(1)}, bf16[24,1664]{1,0:T(8,128)(2,1)S(1)}, u32[]{:S(2)}, u32[]{:S(2)}) collective-permute-start(bf16[24,1664]{1,0:T(8,128)(2,1)S(1)} %concatenate.22), channel_id=1, source_target_pairs={{0,8},{8,0},{16,24},{24,16},{1,9},{9,1},{17,25},{25,17},{2,10},{10... | collective-permute-start | bytes 239624 | tf_op jit(solution)/shard_map/ppermute | solution.py:595
  24.0 1.7 copy-start.4
  27.0 14.1 %collective-permute-start.1 = (bf16[2,24,1536]{2,1,0:T(8,128)(2,1)S(1)}, bf16[2,24,1536]{2,1,0:T(8,128)(2,1)S(1)}, u32[]{:S(2)}, u32[]{:S(2)}) collective-permute-start(bf16[2,24,1536]{2,1,0:T(8,128)(2,1)S(1)} %pad_maximum_fusion.8), channel_id=1, source_target_pairs={{0,16},{8,24},{16,0},{24,8},{1,17},{9,25},{17,1},{25,9},{2,18},{10... | collective-permute-start | bytes 442376 | tf_op jit(solution)/shard_map/ppermute | solution.py:595
  30.1 13.2 %collective-permute-start.6 = (bf16[2,24,1664]{2,1,0:T(8,128)(2,1)S(1)}, bf16[2,24,1664]{2,1,0:T(8,128)(2,1)S(1)}, u32[]{:S(2)}, u32[]{:S(2)}) collective-permute-start(bf16[2,24,1664]{2,1,0:T(8,128)(2,1)S(1)} %pad_maximum_fusion.7), channel_id=1, source_target_pairs={{0,16},{8,24},{16,0},{24,8},{1,17},{9,25},{17,1},{25,9},{2,18},{10... | collective-permute-start | bytes 479240 | tf_op jit(solution)/shard_map/ppermute | solution.py:595
  41.2 6.8 %collective-permute-start.2 = (bf16[2,2,24,1536]{3,2,1,0:T(8,128)(2,1)S(1)}, bf16[2,2,24,1536]{3,2,1,0:T(8,128)(2,1)S(1)}, u32[]{:S(2)}, u32[]{:S(2)}) collective-permute-start(bf16[2,2,24,1536]{3,2,1,0:T(8,128)(2,1)S(1)} %pad_maximum_fusion.6), channel_id=1, source_target_pairs={{0,4},{1,5},{2,6},{3,7},{4,0},{5,1},{6,2},{7,3},{8,12},{9,13},{10,... | collective-permute-start | bytes 884744 | tf_op jit(solution)/shard_map/ppermute | solution.py:595
  43.4 10.5 %collective-permute-start.7 = (bf16[2,2,24,1664]{3,2,1,0:T(8,128)(2,1)S(1)}, bf16[2,2,24,1664]{3,2,1,0:T(8,128)(2,1)S(1)}, u32[]{:S(2)}, u32[]{:S(2)}) collective-permute-start(bf16[2,2,24,1664]{3,2,1,0:T(8,128)(2,1)S(1)} %pad_maximum_fusion.5), channel_id=1, source_target_pairs={{0,2},{1,3},{2,0},{3,1},{4,6},{5,7},{6,4},{7,5},{8,10},{9,11},{10,... | collective-permute-start | bytes 958472 | tf_op jit(solution)/shard_map/ppermute | solution.py:595
  48.1 16.4 %collective-permute-start.3 = (bf16[2,2,2,24,1536]{4,3,2,1,0:T(8,128)(2,1)S(1)}, bf16[2,2,2,24,1536]{4,3,2,1,0:T(8,128)(2,1)S(1)}, u32[]{:S(2)}, u32[]{:S(2)}) collective-permute-start(bf16[2,2,2,24,1536]{4,3,2,1,0:T(8,128)(2,1)S(1)} %pad_maximum_fusion.4), channel_id=1, source_target_pairs={{0,2},{1,3},{2,0},{3,1},{4,6},{5,7},{6,4},{7,5},{8,10},{9,11},{10,... | collective-permute-start | bytes 1769480 | tf_op jit(solution)/shard_map/ppermute | solution.py:595
  54.1 12.2 %collective-permute-start.8 = (bf16[2,2,2,24,1664]{4,3,0,2,1:T(8,128)(2,1)S(1)}, bf16[2,2,2,24,1664]{4,3,0,2,1:T(8,128)(2,1)S(1)}, u32[]{:S(2)}, u32[]{:S(2)}) collective-permute-start(bf16[2,2,2,24,1664]{4,3,0,2,1:T(8,128)(2,1)S(1)} %pad_maximum_fusion.3), channel_id=1, source_target_pairs={{0,4},{1,5},{2,6},{3,7},{4,0},{5,1},{6,2},{7,3},{8,12},{9,13},{10,... | collective-permute-start | bytes 1916936 | tf_op jit(solution)/shard_map/ppermute | solution.py:595
  65.7 16.2 %collective-permute-start.4 = (bf16[2,2,2,2,24,1536]{5,4,3,2,1,0:T(8,128)(2,1)}, bf16[2,2,2,2,24,1536]{5,4,3,2,1,0:T(8,128)(2,1)}, u32[]{:S(2)}, u32[]{:S(2)}) collective-permute-start(bf16[2,2,2,2,24,1536]{5,4,3,2,1,0:T(8,128)(2,1)} %pad_maximum_fusion.2), channel_id=1, source_target_pairs={{0,1},{1,0},{2,3},{3,2},{4,5},{5,4},{6,7},{7,6},{8,9},{9,8},{10,11... | collective-permute-start | bytes 3538952 | tf_op jit(solution)/shard_map/ppermute | solution.py:595
  67.7 17.6 %collective-permute-start.9 = (bf16[2,2,2,2,24,1664]{5,4,1,0,3,2:T(8,128)(2,1)}, bf16[2,2,2,2,24,1664]{5,4,1,0,3,2:T(8,128)(2,1)}, u32[]{:S(2)}, u32[]{:S(2)}) collective-permute-start(bf16[2,2,2,2,24,1664]{5,4,1,0,3,2:T(8,128)(2,1)} %pad_maximum_fusion.1), channel_id=1, source_target_pairs={{0,1},{1,0},{2,3},{3,2},{4,5},{5,4},{6,7},{7,6},{8,9},{9,8},{10,11... | collective-permute-start | bytes 3833864 | tf_op jit(solution)/shard_map/ppermute | solution.py:595
  74.9 42.3 %all-to-all-start.1 = ((bf16[8,256,768]{2,1,0:T(8,128)(2,1)}), bf16[8,256,768]{2,1,0:T(8,128)(2,1)}, u32[]{:S(2)}, u32[]{:S(2)}) async-start(bf16[8,256,768]{2,1,0:T(8,128)(2,1)} %shard_map.324), calls=%async_computation.1 | async-start | bytes 6291456 | tf_op jit(solution)/shard_map/all_to_all | solution.py:699
  87.1 1.5 copy-start.1
  117.3 41.5 %all-to-all-start = ((bf16[8,256,768]{2,1,0:T(8,128)(2,1)}), bf16[8,256,768]{2,1,0:T(8,128)(2,1)S(1)}, u32[]{:S(2)}, u32[]{:S(2)}) async-start(bf16[8,256,768]{2,1,0:T(8,128)(2,1)} %shard_map.323), calls=%async_computation | async-start | bytes 6291456 | tf_op jit(solution)/shard_map/all_to_all | solution.py:705
  120.9 290.2 %reduce-scatter.5.cloned.1.call-start = ((), (), s32[]{:S(2)}) async-start(), calls=%async_computation.7 | async-start | bytes 5898240 | tf_op jit(solution)/shard_map/reduce_scatter | solution.py:714
  158.7 1.7 copy-start.2
  204.4 45.0 %all-to-all-start.2 = ((bf16[8,256,768]{2,1,0:T(8,128)(2,1)}), bf16[8,256,768]{2,1,0:T(8,128)(2,1)}, u32[]{:S(2)}, u32[]{:S(2)}) async-start(bf16[8,256,768]{2,1,0:T(8,128)(2,1)} %bitcast.41), calls=%async_computation.2 | async-start | bytes 6291456 | tf_op jit(solution)/shard_map/all_to_all | solution.py:711
  249.4 5.7 %copy-start.5 = (bf16[768,8]{1,0:T(8,128)(2,1)S(1)}, bf16[768,8]{1,0:T(8,128)(2,1)}, u32[]{:S(2)}) copy-start(bf16[768,8]{1,0:T(8,128)(2,1)} %slice.104.router_ref) | copy-start | bytes 36868
  249.4 6.4 %copy-start.7 = (f32[1,768]{1,0:T(1,128)S(1)}, f32[1,768]{1,0:T(1,128)}, u32[]{:S(2)}) copy-start(f32[1,768]{1,0:T(1,128)} %get-tuple-element.62) | copy-start | bytes 9220
  249.4 7.0 %copy-start.6 = (f32[1,3072]{1,0:T(1,128)S(1)}, f32[1,3072]{1,0:T(1,128)}, u32[]{:S(2)}) copy-start(f32[1,3072]{1,0:T(1,128)} %get-tuple-element.61) | copy-start | bytes 36868
  249.5 42.5 %all-to-all-start.3 = ((bf16[8,256,768]{2,1,0:T(8,128)(2,1)}), bf16[8,256,768]{2,1,0:T(8,128)(2,1)}, u32[]{:S(2)}, u32[]{:S(2)}) async-start(bf16[8,256,768]{2,1,0:T(8,128)(2,1)} %bitcast.164), calls=%async_computation.3 | async-start | bytes 6291456 | tf_op jit(solution)/shard_map/all_to_all | solution.py:718
  254.1 160.5 %reduce-scatter.3.cloned.1.call-start = ((), (), s32[]{:S(2)}) async-start(), calls=%async_computation.6 | async-start | bytes 5898240 | tf_op jit(solution)/shard_map/reduce_scatter | solution.py:721
  257.2 87.7 %collective-permute-start.20 = (f32[2,1,960]{2,0,1:T(2,128)S(1)}, f32[2,1,960]{2,0,1:T(2,128)S(1)}, u32[]{:S(2)}, u32[]{:S(2)}) collective-permute-start(f32[2,1,960]{2,0,1:T(2,128)S(1)} %dynamic-slice_bitcast_fusion.9), channel_id=1, source_target_pairs={{0,16},{8,24},{16,0},{24,8},{1,17},{9,25},{17,1},{25,9},{2,18},{10... | collective-permute-start | bytes 23048 | tf_op jit(solution)/shard_map/ppermute | solution.py:595
  341.1 17.9 %collective-permute-start.15 = (bf16[2,2,2,2,24,1536]{5,4,1,0,2,3:T(8,128)(2,1)}, bf16[2,2,2,2,24,1536]{5,4,1,0,2,3:T(8,128)(2,1)}, u32[]{:S(2)}, u32[]{:S(2)}) collective-permute-start(bf16[2,2,2,2,24,1536]{5,4,1,0,2,3:T(8,128)(2,1)} %bitcast.152), channel_id=1, source_target_pairs={{0,1},{1,0},{2,3},{3,2},{4,5},{5,4},{6,7},{7,6},{8,9},{9,8},{10,11... | collective-permute-start | bytes 3538952 | tf_op jit(solution)/shard_map/ppermute | solution.py:595
  344.3 16.4 %collective-permute-start.10 = (bf16[2,2,2,2,24,1664]{5,4,3,2,1,0:T(8,128)(2,1)}, bf16[2,2,2,2,24,1664]{5,4,3,2,1,0:T(8,128)(2,1)}, u32[]{:S(2)}, u32[]{:S(2)}) collective-permute-start(bf16[2,2,2,2,24,1664]{5,4,3,2,1,0:T(8,128)(2,1)} %dynamic-slice_bitcast_fusion), channel_id=1, source_target_pairs={{0,1},{1,0},{2,3},{3,2},{4,5},{5,4},{6,7},{7,6},{8,9},{9,8},{10,11... | collective-permute-start | bytes 3833864 | tf_op jit(solution)/shard_map/ppermute | solution.py:595
  344.9 7.4 %collective-permute-start.21 = (f32[1,960]{1,0:T(1,128)S(1)}, f32[1,960]{1,0:T(1,128)S(1)}, u32[]{:S(2)}, u32[]{:S(2)}) collective-permute-start(f32[1,960]{1,0:T(1,128)S(1)} %fusion.18), channel_id=1, source_target_pairs={{0,8},{8,0},{16,24},{24,16},{1,9},{9,1},{17,25},{25,17},{2,10},{10... | collective-permute-start | bytes 11528 | tf_op jit(solution)/shard_map/ppermute | solution.py:595
  353.4 3.0 copy-start.3
  356.7 2.4 copy-start
  360.7 15.4 %collective-permute-start.16 = (bf16[2,2,2,24,1536]{4,3,1,0,2:T(8,128)(2,1)S(1)}, bf16[2,2,2,24,1536]{4,3,1,0,2:T(8,128)(2,1)S(1)}, u32[]{:S(2)}, u32[]{:S(2)}) collective-permute-start(bf16[2,2,2,24,1536]{4,3,1,0,2:T(8,128)(2,1)S(1)} %dynamic-slice_bitcast_fusion.2), channel_id=1, source_target_pairs={{0,2},{1,3},{2,0},{3,1},{4,6},{5,7},{6,4},{7,5},{8,10},{9,11},{10,... | collective-permute-start | bytes 1769480 | tf_op jit(solution)/shard_map/ppermute | solution.py:595
  362.5 17.0 %collective-permute-start.11 = (bf16[2,2,2,24,1664]{4,3,2,1,0:T(8,128)(2,1)S(1)}, bf16[2,2,2,24,1664]{4,3,2,1,0:T(8,128)(2,1)S(1)}, u32[]{:S(2)}, u32[]{:S(2)}) collective-permute-start(bf16[2,2,2,24,1664]{4,3,2,1,0:T(8,128)(2,1)S(1)} %dynamic-slice_bitcast_fusion.1), channel_id=1, source_target_pairs={{0,4},{1,5},{2,6},{3,7},{4,0},{5,1},{6,2},{7,3},{8,12},{9,13},{10,... | collective-permute-start | bytes 1916936 | tf_op jit(solution)/shard_map/ppermute | solution.py:595
  376.3 9.0 %collective-permute-start.17 = (bf16[2,2,24,1536]{3,2,1,0:T(8,128)(2,1)S(1)}, bf16[2,2,24,1536]{3,2,1,0:T(8,128)(2,1)S(1)}, u32[]{:S(2)}, u32[]{:S(2)}) collective-permute-start(bf16[2,2,24,1536]{3,2,1,0:T(8,128)(2,1)S(1)} %dynamic-slice_bitcast_fusion.4), channel_id=1, source_target_pairs={{0,4},{1,5},{2,6},{3,7},{4,0},{5,1},{6,2},{7,3},{8,12},{9,13},{10,... | collective-permute-start | bytes 884744 | tf_op jit(solution)/shard_map/ppermute | solution.py:595
  385.4 8.9 %collective-permute-start.18 = (bf16[2,24,1536]{2,1,0:T(8,128)(2,1)S(1)}, bf16[2,24,1536]{2,1,0:T(8,128)(2,1)S(1)}, u32[]{:S(2)}, u32[]{:S(2)}) collective-permute-start(bf16[2,24,1536]{2,1,0:T(8,128)(2,1)S(1)} %dynamic-slice_bitcast_fusion.6), channel_id=1, source_target_pairs={{0,16},{8,24},{16,0},{24,8},{1,17},{9,25},{17,1},{25,9},{2,18},{10... | collective-permute-start | bytes 442376 | tf_op jit(solution)/shard_map/ppermute | solution.py:595
  386.0 8.4 %collective-permute-start.12 = (bf16[2,2,24,1664]{3,2,1,0:T(8,128)(2,1)S(1)}, bf16[2,2,24,1664]{3,2,1,0:T(8,128)(2,1)S(1)}, u32[]{:S(2)}, u32[]{:S(2)}) collective-permute-start(bf16[2,2,24,1664]{3,2,1,0:T(8,128)(2,1)S(1)} %dynamic-slice_bitcast_fusion.3), channel_id=1, source_target_pairs={{0,2},{1,3},{2,0},{3,1},{4,6},{5,7},{6,4},{7,5},{8,10},{9,11},{10,... | collective-permute-start | bytes 958472 | tf_op jit(solution)/shard_map/ppermute | solution.py:595
  394.4 5.1 %collective-permute-start.19 = (bf16[24,1536]{1,0:T(8,128)(2,1)S(1)}, bf16[24,1536]{1,0:T(8,128)(2,1)S(1)}, u32[]{:S(2)}, u32[]{:S(2)}) collective-permute-start(bf16[24,1536]{1,0:T(8,128)(2,1)S(1)} %dynamic-slice_bitcast_fusion.8), channel_id=1, source_target_pairs={{0,8},{8,0},{16,24},{24,16},{1,9},{9,1},{17,25},{25,17},{2,10},{10... | collective-permute-start | bytes 221192 | tf_op jit(solution)/shard_map/ppermute | solution.py:595
  394.6 9.7 %collective-permute-start.13 = (bf16[2,24,1664]{2,1,0:T(8,128)(2,1)S(1)}, bf16[2,24,1664]{2,1,0:T(8,128)(2,1)S(1)}, u32[]{:S(2)}, u32[]{:S(2)}) collective-permute-start(bf16[2,24,1664]{2,1,0:T(8,128)(2,1)S(1)} %dynamic-slice_bitcast_fusion.5), channel_id=1, source_target_pairs={{0,16},{8,24},{16,0},{24,8},{1,17},{9,25},{17,1},{25,9},{2,18},{10... | collective-permute-start | bytes 479240 | tf_op jit(solution)/shard_map/ppermute | solution.py:595
  404.4 4.5 %collective-permute-start.14 = (bf16[24,1664]{1,0:T(8,128)(2,1)S(1)}, bf16[24,1664]{1,0:T(8,128)(2,1)S(1)}, u32[]{:S(2)}, u32[]{:S(2)}) collective-permute-start(bf16[24,1664]{1,0:T(8,128)(2,1)S(1)} %dynamic-slice_bitcast_fusion.7), channel_id=1, source_target_pairs={{0,8},{8,0},{16,24},{24,16},{1,9},{9,1},{17,25},{25,17},{2,10},{10... | collective-permute-start | bytes 239624 | tf_op jit(solution)/shard_map/ppermute | solution.py:595
Sparse Core Ops, SparseCore 0:
  204.5 87.0 reduce-scatter.4
  294.0 85.8 reduce-scatter.2
